TPU v7x, 32 devices: a whole 2x2x4 slice. The times are simulated.
32 devices in a mesh: sample: 4 (over z), space: 8 (over y, x, core).
Axes of the slice: x: 2, y: 2, z: 4, core: 2. Of those that a mesh axis runs over, the one named last changes fastest.
Arguments:
- concentration: float32 [4, 4, 512, 512], P('sample', None, 'space'), may hold values from -12 to 12
- classes: int32 [4, 4, 512, 512], P('sample', None, 'space'), may hold values from 0 to 15
- conductivity: float32 [16], replicated, may hold values from 0.1 to 10
- wells: int32 [2, 64], replicated, may hold values from 0 to 511
- control: float32 [64], replicated, may hold values from -40 to 40
Outputs:
- final_conc: float32 [4, 4, 512, 512], P('sample', None, 'space')
- adjoint_start: float32 [4, 4, 512, 512], P('sample', None, 'space')
- gradient: float32 [64], replicated
All inputs are finite; a program needn't handle non-finite values.
Results may differ from a plain program's by a relative error of at most 0.0003.
Values sent between devices are 32-bit elements; how exact they have to be, the bound alone decides.
A program may use at most 128 MiB of HBM per device.

v0:
```python
import functools
import jax
import jax.numpy as jnp
from jax import lax
from jax.experimental import pallas as pl
from jax.experimental.pallas import tpu as pltpu
from jax.sharding import PartitionSpec as P

spread_along = 200.0
drift_along = 6.0
spread_across = 200.0
drift_across = 3.0
spread_depth = 2.0
drift_depth = 0.0
aversion = 0.5
epsilon = 1e-06


def offset(values, amount, direction, filler):
    length = values.shape[direction]
    distance = abs(amount)
    margin = list(values.shape)
    margin[direction] = distance
    padding = jnp.full(margin, filler, values.dtype)
    if amount > 0:
        retained = lax.slice_in_dim(values, 0, length - distance, axis=direction)
        return jnp.concatenate([padding, retained], axis=direction)
    retained = lax.slice_in_dim(values, distance, length, axis=direction)
    return jnp.concatenate([retained, padding], axis=direction)


def line_terms(conduct, direction, spread, advection):
    following = offset(conduct, -1, direction, 0.0)
    face_ahead = 2.0 * conduct * following / (conduct + following)
    behind = offset(face_ahead, 1, direction, 0.0)
    subdiag = offset(-(spread * face_ahead + advection), 1, direction, 0.0)
    middle = 1.0 + spread * (behind + face_ahead) + advection
    superdiag = -spread * face_ahead
    return (subdiag, middle, superdiag)


def factor_lines(terms, direction):
    subdiag, middle, superdiag = terms
    length = middle.shape[direction]
    levels = []
    stride = 1
    while stride < length:
        middle_before = offset(middle, stride, direction, 1.0)
        middle_after = offset(middle, -stride, direction, 1.0)
        weight_below = -subdiag / middle_before
        weight_above = -superdiag / middle_after
        new_middle = (
            middle
            + weight_below * offset(superdiag, stride, direction, 0.0)
            + weight_above * offset(subdiag, -stride, direction, 0.0)
        )
        subdiag = weight_below * offset(subdiag, stride, direction, 0.0)
        superdiag = weight_above * offset(superdiag, -stride, direction, 0.0)
        middle = new_middle
        levels.append((weight_below, weight_above))
        stride = stride * 2
    return (levels, middle)


def solve_lines(values, factored, direction):
    levels, middle = factored
    stride = 1
    for weight_below, weight_above in levels:
        values = (
            values
            + weight_below * offset(values, stride, direction, 0.0)
            + weight_above * offset(values, -stride, direction, 0.0)
        )
        stride = stride * 2
    return values / middle


def solve_back(values, factored, direction):
    levels, middle = factored
    values = values / middle
    for depth_level in range(len(levels) - 1, -1, -1):
        weight_below, weight_above = levels[depth_level]
        stride = 2**depth_level
        values = (
            values
            + offset(weight_below * values, -stride, direction, 0.0)
            + offset(weight_above * values, stride, direction, 0.0)
        )
    return values


def pack_lines(values):
    planes, rows_here, length = values.shape
    count = lax.axis_size("space")
    return values.reshape(planes, rows_here, count, length // count).transpose(0, 2, 3, 1)


def unpack_lines(values):
    return values.reshape(values.shape[0], values.shape[2], values.shape[3])


def into_columns(values):
    return unpack_lines(
        lax.all_to_all(pack_lines(values), "space", split_axis=1, concat_axis=3, tiled=True)
    )


def into_rows(values):
    return unpack_lines(
        lax.all_to_all(pack_lines(values), "space", split_axis=1, concat_axis=3, tiled=True)
    )


def well_sum(column_sum, hits_rows, hits_columns):
    picked = jnp.dot(
        hits_rows, column_sum, precision=lax.Precision.HIGHEST, preferred_element_type=jnp.float32
    )
    return jnp.sum(picked * hits_columns, axis=1)


def per_device(concentration, classes, conductivity, wells, control):
    start_state = concentration[0]
    class_cells = classes[0]
    grid_cells = start_state.shape[2]
    block_size = start_state.shape[1]
    position = lax.axis_index("space")
    conduct_rows = jnp.zeros(class_cells.shape, jnp.float32)
    for class_label in range(conductivity.shape[0]):
        conduct_rows = conduct_rows + jnp.where(
            class_cells == class_label, conductivity[class_label], 0.0
        )
    conduct_columns = unpack_lines(
        lax.all_to_all(pack_lines(conduct_rows), "space", split_axis=1, concat_axis=3, tiled=True)
    )
    along_factor = factor_lines(line_terms(conduct_columns, 2, spread_along, drift_along), 2)
    across_factor = factor_lines(line_terms(conduct_rows, 2, spread_across, drift_across), 2)
    depth_rows = factor_lines(line_terms(conduct_rows, 0, spread_depth, drift_depth), 0)
    local_index = position * block_size + lax.iota(jnp.int32, block_size)
    all_index = lax.iota(jnp.int32, grid_cells)
    hits_first_local = (wells[0][:, None] == local_index[None, :]).astype(jnp.float32)
    hits_second_all = (wells[1][:, None] == all_index[None, :]).astype(jnp.float32)
    hits_second_local = (wells[1][:, None] == local_index[None, :]).astype(jnp.float32)
    hits_first_all = (wells[0][:, None] == all_index[None, :]).astype(jnp.float32)
    source = jnp.dot(
        hits_first_local.T,
        control[:, None] * hits_second_all,
        precision=lax.Precision.HIGHEST,
        preferred_element_type=jnp.float32,
    )
    depth_columns = factor_lines(line_terms(conduct_columns, 0, spread_depth, drift_depth), 0)
    current = into_columns(start_state + source[None])
    current = solve_lines(current, along_factor, 2)
    current = solve_lines(current, depth_columns, 0)
    current = into_rows(current)
    current = solve_lines(current, across_factor, 2)
    current = current + source[None]
    current = solve_lines(current, across_factor, 2)
    current = solve_lines(current, depth_rows, 0)
    final_state = solve_lines(into_columns(current), along_factor, 2)
    misfit_part = 0.5 * jnp.sum(final_state * final_state)
    second_adjoint = solve_back(final_state, along_factor, 2)
    second_adjoint = solve_back(second_adjoint, depth_columns, 0)
    second_adjoint = solve_back(into_rows(second_adjoint), across_factor, 2)
    first_adjoint = solve_back(second_adjoint, across_factor, 2)
    first_adjoint = solve_back(first_adjoint, depth_rows, 0)
    adjoint_state = solve_back(into_columns(first_adjoint), along_factor, 2)
    well_terms = well_sum(jnp.sum(second_adjoint, axis=0), hits_first_local, hits_second_all)
    well_terms = well_terms + well_sum(
        jnp.sum(adjoint_state, axis=0), hits_second_local, hits_first_all
    )
    sample_count = lax.axis_size("sample")
    own_misfit = lax.psum(misfit_part, "space")
    misfit_total = lax.psum(own_misfit, "sample")
    average = misfit_total / sample_count
    weight = (1.0 + aversion * (own_misfit - average) / (average + epsilon)) / sample_count
    gradient = lax.psum(weight * well_terms, ("sample", "space"))
    return (final_state[None], adjoint_state[None], gradient)


LANES = 128
SUBLANES = 8
UNROLL = 8
MESH = pl.DeviceIdType.MESH
EXACT = lax.Precision.HIGHEST


def steps(count, body, carry):
    def turn(t, state):
        for k in range(UNROLL):
            state = body(t * UNROLL + k, state)
        return state

    return lax.fori_loop(0, count // UNROLL, turn, carry)


def rows_at(i, pieces, length):
    return pl.ds(i, pieces, stride=length)


def take(ref, at):
    return jnp.concatenate([ref[j, at, :] for j in range(ref.shape[0])], axis=1)


def put(ref, at, value):
    for j in range(ref.shape[0]):
        ref[j, at, :] = value[:, j * LANES : (j + 1) * LANES]


def width(ref):
    return ref.shape[0] * LANES


def factor_blocks(cond, factors, pieces, length, before, beyond, spread, drift):
    low, up, inv, from_first, to_first = factors
    shape = (pieces, width(cond))

    def keep(i, d, ahead, state):
        eta, eta_t, corner = state
        r = 1.0 / d
        u = -spread * ahead * r
        lo = -(spread * ahead + drift) * r
        at = rows_at(i, pieces, length)
        put(low, at, lo)
        put(up, at, u)
        put(inv, at, r)
        first = eta * r
        put(from_first, at, first)
        put(to_first, at, eta_t * r)
        return u, (-lo * eta, -u * eta_t, corner + first * eta_t)

    def body(i, state):
        here, behind, u, rest = state
        after = take(cond, rows_at(jnp.minimum(i + 1, length - 1), pieces, length))
        ahead = 2.0 * here * after / (here + after)
        ahead = jnp.where(i == length - 1, last_face, ahead)
        d = 1.0 + spread * (behind + ahead) + drift + (spread * behind + drift) * u
        u, rest = keep(i, d, ahead, rest)
        return after, ahead, u, rest

    first_row = take(cond, rows_at(0, pieces, length))
    last_face = beyond(first_row, take(cond, rows_at(length - 1, pieces, length)))
    ones = jnp.ones(shape, jnp.float32)
    zeros = jnp.zeros(shape, jnp.float32)
    state = steps(length, body, (first_row, before, zeros, (ones, ones, zeros)))
    at = rows_at(length - 1, pieces, length)
    return state[3][2], take(from_first, at), take(to_first, at), take(inv, at), last_face


def sweep_down(values, out, low, inv, weights, pieces, length):
    def body(i, state):
        y, lo, total = state
        at = rows_at(i, pieces, length)
        y = take(values, at) - lo * y
        put(out, at, y * take(inv, at))
        return y, take(low, at), total + take(weights, at) * y

    zeros = jnp.zeros((pieces, width(values)), jnp.float32)
    _, _, total = steps(length, body, (zeros, zeros, zeros))
    return total, take(out, rows_at(length - 1, pieces, length))


def sweep_up(held, out, up, spike, incoming, following, pieces, length):
    def body(k, x):
        at = rows_at(length - 1 - k, pieces, length)
        x = take(held, at) - take(spike, at) * incoming - take(up, at) * x
        put(out, at, x)
        return x

    steps(length, body, following)


def joint_terms(vf, vl, wf, wl, beta):
    r = 1.0 / (1.0 - vf * beta)
    s = vl * beta * r
    return s, vl + s * vf, r, r * vf, r * wf, wl + s * wf


def tile_transpose(source, target):
    for i in range(target.shape[0]):
        for j in range(source.shape[0]):
            target[i, j * LANES : (j + 1) * LANES, :] = source[j, i * LANES : (i + 1) * LANES, :].T


def kernel(
    parts, samples, planes,
    conc, classes, conductivity, wells, control,
    final_out, adjoint_out, gradient_out,
    cond, cond_t, xl, xu, xi, xe, xf, yl, yu, yi, ye, yf, zu, zi,
    field, held, field_t, held_t, later_t, source_t, final_t, adjoint_t,
    hits_x, hits_y, halo_send, halo, corner, joint_x, joint_y, ends, ps, qs,
    landed, part_sum, sample_sum, term_sum, sample_term,
    send_sem, recv_sem, bulk_send, bulk_recv, sample_send, sample_recv, halo_ssem, halo_rsem,
):
    me = lax.axis_index("space")
    own = lax.axis_index("sample")
    block = conc.shape[0] // planes
    grid_cells = conc.shape[1]
    length_t = grid_cells // SUBLANES
    wide = conc.shape[0]

    barrier = pltpu.get_barrier_semaphore()

    def peer(k):
        return {"space": lax.rem(me + k, parts)}

    def partner(k):
        return {"sample": lax.rem(own + k, samples)}

    for k in range(1, parts):
        pl.semaphore_signal(barrier, inc=1, device_id=peer(k), device_id_type=MESH)
    for k in range(1, samples):
        pl.semaphore_signal(barrier, inc=1, device_id=partner(k), device_id_type=MESH)

    def spread_out(ref, phase):
        copies = []
        for k in range(1, parts):
            copy = pltpu.make_async_remote_copy(
                src_ref=ref.at[me], dst_ref=ref.at[me],
                send_sem=send_sem.at[phase, k], recv_sem=recv_sem.at[phase, k],
                device_id=peer(k), device_id_type=MESH)
            copy.start()
            copies.append(copy)
        return copies

    def spread_samples(ref, phase):
        copies = []
        for k in range(1, samples):
            copy = pltpu.make_async_remote_copy(
                src_ref=ref.at[own], dst_ref=ref.at[own],
                send_sem=sample_send.at[phase, k], recv_sem=sample_recv.at[phase, k],
                device_id=partner(k), device_id_type=MESH)
            copy.start()
            copies.append(copy)
        return copies

    def send_blocks(ref, phase):
        copies = []
        for k in range(1, parts):
            to = lax.rem(me + k, parts)
            copy = pltpu.make_async_remote_copy(
                src_ref=ref.at[:, pl.ds(pl.multiple_of(to * block, block), block)],
                dst_ref=landed.at[phase, me],
                send_sem=bulk_send.at[phase, k], recv_sem=bulk_recv.at[phase, k],
                device_id=peer(k), device_id_type=MESH)
            copy.start()
            copies.append(copy)
        landed[phase, me] = ref[:, pl.ds(pl.multiple_of(me * block, block), block), :]
        return copies

    pending = []

    def arrive(copies):
        for copy in copies:
            copy.wait_recv()
        pending.extend(copies)

    def fill(t, _):
        at = pl.ds(pl.multiple_of(t * SUBLANES, SUBLANES), SUBLANES)
        labels = classes[at, :]
        values = jnp.full(labels.shape, conductivity[0], jnp.float32)
        for label in range(1, conductivity.shape[0]):
            values = jnp.where(labels == label, conductivity[label], values)
        put(cond, at, values)
        return 0

    lax.fori_loop(0, wide // SUBLANES, fill, 0)
    halo_send[0] = take(cond, rows_at(block - 1, planes, block))
    halo_send[1] = take(cond, rows_at(0, planes, block))
    pl.semaphore_wait(barrier, parts - 1 + samples - 1)
    halo_copies = []
    for side, k in ((0, 1), (1, parts - 1)):
        copy = pltpu.make_async_remote_copy(
            src_ref=halo_send.at[side], dst_ref=halo.at[side],
            send_sem=halo_ssem.at[side], recv_sem=halo_rsem.at[side],
            device_id=peer(k), device_id_type=MESH)
        copy.start()
        halo_copies.append(copy)

    def factor_depth(t, _):
        start = t * SUBLANES
        here = take(cond, pl.ds(pl.multiple_of(start, SUBLANES), SUBLANES))
        behind = jnp.zeros(here.shape, jnp.float32)
        u = behind
        for z in range(planes):
            if z < planes - 1:
                after = take(cond, pl.ds(pl.multiple_of((z + 1) * block + start, SUBLANES), SUBLANES))
                ahead = 2.0 * here * after / (here + after)
            else:
                after, ahead = here, jnp.zeros(here.shape, jnp.float32)
            r = 1.0 / (1.0 + spread_depth * (behind + ahead) + spread_depth * behind * u)
            u = -spread_depth * ahead * r
            at = pl.ds(pl.multiple_of(z * block + start, SUBLANES), SUBLANES)
            put(zi, at, r)
            put(zu, at, u)
            here, behind = after, ahead
        return 0

    lax.fori_loop(0, block // SUBLANES, factor_depth, 0)
    tile_transpose(cond, cond_t)

    x_row = lax.broadcasted_iota(jnp.int32, hits_x.shape, 0) % block + me * block
    hits_x[...] = jnp.where(x_row == wells[0:1, :], 1.0, 0.0)
    y_row = lax.broadcasted_iota(jnp.int32, hits_y.shape, 0)
    hits_y[...] = jnp.where(y_row == wells[1:2, :], 1.0, 0.0)
    across_last = (((1,), (1,)), ((), ()))
    source = lax.dot_general(
        hits_x[0:block, :] * control[...], hits_y[...], across_last,
        precision=EXACT, preferred_element_type=jnp.float32)
    for z in range(planes):
        cut = slice(z * block, (z + 1) * block)
        put(field, cut, conc[cut, :] + source)

    arrive(halo_copies)
    x_factors = (xl, xu, xi, xe, xf)
    not_first = (me > 0).astype(jnp.float32)
    not_last = (me < parts - 1).astype(jnp.float32)
    first_row = take(cond, rows_at(0, planes, block))
    face_before = not_first * 2.0 * halo[0] * first_row / (halo[0] + first_row)

    def beyond_x(first, last):
        return not_last * 2.0 * halo[1] * last / (halo[1] + last)

    corners = factor_blocks(
        cond, x_factors, planes, block, face_before, beyond_x, spread_along, drift_along)
    gff, glf, gfl, gll, face_ahead = corners
    for j, value in enumerate((gff, glf, gfl, gll, face_before, face_ahead)):
        corner[me, j * planes : (j + 1) * planes, :] = value
    corner_copies = spread_out(corner, 0)

    def ends_out(phase, first, last):
        ends[phase, me, 0:planes, :] = first
        ends[phase, me, planes : 2 * planes, :] = last
        copies = []
        for k in range(1, parts):
            copy = pltpu.make_async_remote_copy(
                src_ref=ends.at[phase, me], dst_ref=ends.at[phase, me],
                send_sem=send_sem.at[phase + 1, k], recv_sem=recv_sem.at[phase + 1, k],
                device_id=peer(k), device_id_type=MESH)
            copy.start()
            copies.append(copy)
        return copies

    def start_x(values, out, phase, flipped):
        low, weights = (xu, xe) if flipped else (xl, xf)
        first, last = sweep_down(values, out, low, xi, weights, planes, block)
        return ends_out(phase, first, last)

    def finish_x(copies, inner, out, phase, flipped):
        arrive(copies)
        way = 1 if flipped else 0
        joint = lambda b, j: joint_x[way, b, j * planes : (j + 1) * planes, :]
        firsts = [ends[phase, b, 0:planes, :] for b in range(parts)]
        alphas = []
        alpha = None
        for b in range(parts):
            last = ends[phase, b, planes : 2 * planes, :]
            alpha = last if b == 0 else last + joint(b, 0) * firsts[b] - joint(b, 1) * alpha
            alphas.append(alpha)
        zero = jnp.zeros_like(firsts[0])
        ps[parts] = zero
        qs[0] = zero
        p = zero
        for b in range(parts - 1, -1, -1):
            if b < parts - 1:
                qs[b + 1] = alphas[b] - joint(b, 5) * p
            value = joint(b, 2) * firsts[b] - joint(b, 4) * p
            if b > 0:
                value = value - joint(b, 3) * alphas[b - 1]
            p = value
            ps[b] = p
        coupling = -spread_along * face_before if flipped else -(spread_along * face_before + drift_along)
        incoming = coupling * qs[me]
        up, spike = (xl, xf) if flipped else (xu, xe)
        sweep_up(inner, out, up, spike, incoming, ps[me + 1], planes, block)

    x1 = start_x(field, held, 0, False)

    row = lax.broadcasted_iota(jnp.int32, (SUBLANES, wide), 0)
    y_factors = (yl, yu, yi, ye, yf)
    y_first = take(cond_t, rows_at(0, SUBLANES, length_t))
    y_last = take(cond_t, rows_at(length_t - 1, SUBLANES, length_t))
    last_before = pltpu.roll(y_last, 1, 0)
    y_before = jnp.where(row == 0, 0.0, 2.0 * last_before * y_first / (last_before + y_first))

    def beyond_y(first, last):
        after = pltpu.roll(first, SUBLANES - 1, 0)
        return jnp.where(row == SUBLANES - 1, 0.0, 2.0 * last * after / (last + after))

    gff, glf, gfl, gll, y_ahead = factor_blocks(
        cond_t, y_factors, SUBLANES, length_t, y_before, beyond_y, spread_across, drift_across)
    y_couplings = []
    for way in range(2):
        a = jnp.where(row == 0, 0.0, -(spread_across * y_before + drift_across))
        a_next = jnp.where(row == SUBLANES - 1, 0.0, -(spread_across * y_ahead + drift_across))
        c = -spread_across * y_before
        c_next = -spread_across * y_ahead
        if way == 0:
            vf, vl, wf, wl = a * gff, a * glf, c_next * gfl, c_next * gll
            y_couplings.append(a)
        else:
            vf, vl, wf, wl = c * gff, c * gfl, a_next * glf, a_next * gll
            y_couplings.append(c)
        beta = jnp.zeros((1, wide), jnp.float32)
        for b in range(SUBLANES):
            cut = slice(b, b + 1)
            terms = joint_terms(vf[cut], vl[cut], wf[cut], wl[cut], beta)
            beta = terms[5]
            for j, value in enumerate(terms):
                joint_y[way, j, b : b + 1, :] = value
        ahead = jnp.where(row == 0, 0.0, -joint_y[way, 1])
        back = -joint_y[way, 4]
        back = jnp.where(row == SUBLANES - 1, 0.0, back)
        for level, distance in enumerate((1, 2, 4)):
            joint_y[way, 6 + level] = ahead
            joint_y[way, 9 + level] = back
            ahead = jnp.where(row < 2 * distance, 0.0, ahead * pltpu.roll(ahead, distance, 0))
            back = jnp.where(
                row >= SUBLANES - 2 * distance, 0.0,
                back * pltpu.roll(back, SUBLANES - distance, 0))

    def solve_y(values, inner, out, flipped):
        way = 1 if flipped else 0
        low, weights = (yu, ye) if flipped else (yl, yf)
        up, spike = (yl, yf) if flipped else (yu, ye)
        first, last = sweep_down(values, inner, low, yi, weights, SUBLANES, length_t)
        alpha = last + joint_y[way, 0] * first
        for level, distance in enumerate((1, 2, 4)):
            alpha = alpha + joint_y[way, 6 + level] * pltpu.roll(alpha, distance, 0)
        alpha_before = jnp.where(row == 0, 0.0, pltpu.roll(alpha, 1, 0))
        p = joint_y[way, 2] * first - joint_y[way, 3] * alpha_before
        for level, distance in enumerate((1, 2, 4)):
            p = p + joint_y[way, 9 + level] * pltpu.roll(p, SUBLANES - distance, 0)
        p_next = jnp.where(row == SUBLANES - 1, 0.0, pltpu.roll(p, SUBLANES - 1, 0))
        q = alpha - joint_y[way, 5] * p_next
        q_before = jnp.where(row == 0, 0.0, pltpu.roll(q, 1, 0))
        incoming = y_couplings[way] * q_before
        sweep_up(inner, out, up, spike, incoming, p_next, SUBLANES, length_t)

    def solve_z(values):
        def body(t, _):
            start = t * SUBLANES
            ats = [pl.ds(pl.multiple_of(z * block + start, SUBLANES), SUBLANES) for z in range(planes)]
            ys = [take(values, ats[0])]
            us = [take(zu, at) for at in ats]
            for z in range(1, planes):
                ys.append(take(values, ats[z]) - us[z - 1] * ys[-1])
            x = ys[-1] * take(zi, ats[-1])
            put(values, ats[-1], x)
            for z in range(planes - 2, -1, -1):
                x = ys[z] * take(zi, ats[z]) - us[z] * x
                put(values, ats[z], x)
            return 0

        lax.fori_loop(0, block // SUBLANES, body, 0)

    put(source_t, slice(None), lax.dot_general(
        hits_y[...] * control[...], hits_x[...], across_last,
        precision=EXACT, preferred_element_type=jnp.float32))

    arrive(corner_copies)
    corner_of = lambda b, j: corner[b, j * planes : (j + 1) * planes, :]
    for way in range(2):
        beta = jnp.zeros((planes, grid_cells), jnp.float32)
        for b in range(parts):
            gff, glf, gfl, gll, behind, ahead = [corner_of(b, j) for j in range(6)]
            a = -(spread_along * behind + drift_along) if b > 0 else jnp.zeros_like(behind)
            a_next = -(spread_along * ahead + drift_along) if b < parts - 1 else jnp.zeros_like(ahead)
            c, c_next = -spread_along * behind, -spread_along * ahead
            if way == 0:
                terms = joint_terms(a * gff, a * glf, c_next * gfl, c_next * gll, beta)
            else:
                terms = joint_terms(c * gff, c * gfl, a_next * glf, a_next * gll, beta)
            beta = terms[5]
            for j, value in enumerate(terms):
                joint_x[way, b, j * planes : (j + 1) * planes, :] = value

    finish_x(x1, held, field, 0, False)
    solve_z(field)
    tile_transpose(field, field_t)
    solve_y(field_t, held_t, field_t, False)

    field_t[...] = field_t[...] + source_t[...]
    solve_y(field_t, held_t, field_t, False)
    tile_transpose(field_t, field)
    solve_z(field)
    x2 = start_x(field, held, 1, False)
    finish_x(x2, held, field, 1, False)

    x3 = start_x(field, held, 2, True)
    tile_transpose(field, final_t)
    final_copies = send_blocks(final_t, 0)

    def squares(t, total):
        value = take(field, pl.ds(pl.multiple_of(t * SUBLANES, SUBLANES), SUBLANES))
        return total + value * value

    total = lax.fori_loop(
        0, wide // SUBLANES, squares, jnp.zeros((SUBLANES, grid_cells), jnp.float32))
    part_sum[me] = 0.5 * sum(
        total[:, j : j + LANES] for j in range(0, grid_cells, LANES))
    misfit_copies = spread_out(part_sum, 5)

    finish_x(x3, held, field, 2, True)
    solve_z(field)
    tile_transpose(field, field_t)
    solve_y(field_t, held_t, later_t, True)
    arrive(misfit_copies)
    sample_sum[own] = sum(part_sum[b] for b in range(parts))
    sample_copies = spread_samples(sample_sum, 0)

    solve_y(later_t, held_t, field_t, True)
    tile_transpose(field_t, field)
    solve_z(field)
    x4 = start_x(field, held, 3, True)
    half = lax.broadcasted_iota(jnp.int32, (block, LANES), 1) < block

    def assemble(phase, out):
        for j in range(parts // 2):
            for w in range(planes // 2):
                left = landed[phase, 2 * j, w]
                right = landed[phase, 2 * j + 1, w]
                cut = slice(j * LANES, (j + 1) * LANES)
                out[2 * w, :, cut] = jnp.where(half, left, pltpu.roll(right, block, 1))
                out[2 * w + 1, :, cut] = jnp.where(half, pltpu.roll(left, block, 1), right)

    arrive(final_copies)
    assemble(0, final_out)
    finish_x(x4, held, field, 3, True)
    tile_transpose(field, adjoint_t)
    adjoint_copies = send_blocks(adjoint_t, 1)

    arrive(sample_copies)
    misfits = [jnp.sum(sample_sum[s], keepdims=True) for s in range(samples)]
    average = sum(misfits) / samples
    own_misfit = jnp.sum(sample_sum[own], keepdims=True)
    weight = (1.0 + aversion * (own_misfit - average) / (average + epsilon)) / samples
    picked = jnp.dot(
        take(later_t, slice(None)) + take(adjoint_t, slice(None)), hits_x[...],
        precision=EXACT, preferred_element_type=jnp.float32) * hits_y[...]
    picked = picked.reshape(grid_cells // SUBLANES, SUBLANES, picked.shape[1])
    term_sum[me] = weight * jnp.sum(picked, axis=0)
    term_copies = spread_out(term_sum, 6)
    arrive(term_copies)
    sample_term[own] = sum(term_sum[b] for b in range(parts))
    gradient_copies = spread_samples(sample_term, 1)
    arrive(gradient_copies)
    gradient_out[...] = jnp.sum(sum(sample_term[s] for s in range(samples)), axis=0, keepdims=True)

    arrive(adjoint_copies)
    assemble(1, adjoint_out)
    for copy in pending:
        copy.wait_send()


def fused(parts, samples, concentration, classes, conductivity, wells, control):
    _, planes, block, grid_cells = concentration.shape
    wide = planes * block
    count = wells.shape[1]
    f32 = jnp.float32
    vmem = lambda *shape: pltpu.VMEM(shape, f32)
    flat, turned = (grid_cells // LANES, wide, LANES), (wide // LANES, grid_cells, LANES)
    dma = pltpu.SemaphoreType.DMA
    scratch = [vmem(*flat), vmem(*turned)]
    scratch += [vmem(*flat)] * 5 + [vmem(*turned)] * 5 + [vmem(*flat)] * 2
    scratch += [vmem(*flat)] * 2 + [vmem(*turned)] * 6
    scratch += [
        vmem(wide, count), vmem(grid_cells, count),
        vmem(2, planes, grid_cells), vmem(2, planes, grid_cells),
        vmem(parts, 6 * planes, grid_cells),
        vmem(2, parts, 6 * planes, grid_cells),
        vmem(2, 12, SUBLANES, wide),
        vmem(4, parts, 2 * planes, grid_cells),
        vmem(parts + 1, planes, grid_cells), vmem(parts + 1, planes, grid_cells),
        vmem(2, parts, wide // LANES, block, LANES),
        vmem(parts, SUBLANES, LANES), vmem(samples, SUBLANES, LANES),
        vmem(parts, SUBLANES, count), vmem(samples, SUBLANES, count),
        dma((7, parts)), dma((7, parts)), dma((2, parts)), dma((2, parts)),
        dma((2, samples)), dma((2, samples)), dma((2,)), dma((2,)),
    ]
    on_vmem = pl.BlockSpec(memory_space=pltpu.VMEM)
    on_smem = pl.BlockSpec(memory_space=pltpu.SMEM)
    out = jax.ShapeDtypeStruct((planes, block, grid_cells), f32)
    final, adjoint, gradient = pl.pallas_call(
        functools.partial(kernel, parts, samples, planes),
        out_shape=(out, out, jax.ShapeDtypeStruct((1, count), f32)),
        in_specs=[on_vmem, on_vmem, on_smem, on_vmem, on_vmem],
        out_specs=(on_vmem, on_vmem, on_vmem),
        scratch_shapes=scratch,
        compiler_params=pltpu.CompilerParams(
            collective_id=0, has_side_effects=True, vmem_limit_bytes=48 * 1024 * 1024),
    )(
        concentration.reshape(wide, grid_cells), classes.reshape(wide, grid_cells), conductivity, wells,
        control.reshape(1, count))
    return final[None], adjoint[None], gradient.reshape(count)


def choose(axes, concentration, classes, conductivity, wells, control):
    parts, samples = axes["space"], axes["sample"]
    _, planes, block, grid_cells = concentration.shape
    fits = (
        2 * block == LANES and planes % 2 == 0 and parts % 2 == 0 and parts > 1
        and parts * block == grid_cells and grid_cells % LANES == 0
        and (planes * block) % LANES == 0
    )
    if fits:
        return fused(parts, samples, concentration, classes, conductivity, wells, control)
    return per_device(concentration, classes, conductivity, wells, control)


def solution(mesh):
    placed = (P("sample", None, "space", None), P("sample", None, "space", None), P(), P(), P())
    return jax.shard_map(
        functools.partial(choose, mesh.shape),
        mesh=mesh,
        in_specs=placed,
        out_specs=(P("sample", None, "space", None), P("sample", None, "space", None), P()),
        check_vma=False,
    )
```

profile of v0, /device:TPU:0, one launch (start us, length us, event | category | flops | bytes accessed | tf_op | source)
XLA Modules:
  0.0 78.9 jit_solution(2822583277292943373)
XLA Ops:
  0.6 0.0 copy-start.4
  0.6 0.0 copy-start.2
  0.7 0.0 copy-start.3
  0.7 0.6 copy-done.4
  1.3 0.0 copy-done.2
  1.3 0.0 copy-done.3
  1.3 0.0 copy-start
  1.3 1.0 %copy-done = f32[1,4,64,512]{3,2,1,0:T(8,128)S(1)} copy-done((f32[1,4,64,512]{3,2,1,0:T(8,128)S(1)}, f32[1,4,64,512]{3,2,1,0:T(8,128)}, u32[]{:S(2)}) %copy-start) | copy-done | bytes 524312
  2.4 0.0 copy-start.1
  2.4 1.0 %copy-done.1 = s32[1,4,64,512]{3,2,1,0:T(8,128)S(1)} copy-done((s32[1,4,64,512]{3,2,1,0:T(8,128)S(1)}, s32[1,4,64,512]{3,2,1,0:T(8,128)}, u32[]{:S(2)}) %copy-start.1) | copy-done | bytes 524312
  3.4 73.4 %shard_map.76 = (f32[4,64,512]{2,1,0:T(8,128)S(1)}, f32[4,64,512]{2,1,0:T(8,128)S(1)}, f32[1,64]{1,0:T(1,128)S(1)}) custom-call(f32[256,512]{1,0:T(8,128)S(1)} %bitcast.6, s32[256,512]{1,0:T(8,128)S(1)} %bitcast.7, f32[16]{0:T(128)S(1)} %copy-done.3, s32[2,64]{1,0:T(2,128)S(1)} %copy-done.2, f32[1,64]{1,0:T(1,128)S(1)} %bitcast.10), custom_call_target="tpu_custom_call" | custom-call | tf_op jit(solution)/shard_map/pallas_call | solution.py:683
  76.8 0.8 %copy.11 = f32[1,4,64,512]{3,2,1,0:T(8,128)} copy(f32[1,4,64,512]{3,2,1,0:T(8,128)S(1)} %bitcast.9) | data formatting | bytes 1048576
  77.6 0.8 %copy.12 = f32[1,4,64,512]{3,2,1,0:T(8,128)} copy(f32[1,4,64,512]{3,2,1,0:T(8,128)S(1)} %bitcast.8) | data formatting | bytes 1048576
  78.4 0.5 copy.13
Async XLA Ops:
  0.6 0.7 copy-start.4
  0.6 0.7 copy-start.2
  0.7 0.7 copy-start.3
  1.3 1.0 %copy-start = (f32[1,4,64,512]{3,2,1,0:T(8,128)S(1)}, f32[1,4,64,512]{3,2,1,0:T(8,128)}, u32[]{:S(2)}) copy-start(f32[1,4,64,512]{3,2,1,0:T(8,128)} %param.5) | copy-start | bytes 1572868
  2.4 1.0 %copy-start.1 = (s32[1,4,64,512]{3,2,1,0:T(8,128)S(1)}, s32[1,4,64,512]{3,2,1,0:T(8,128)}, u32[]{:S(2)}) copy-start(s32[1,4,64,512]{3,2,1,0:T(8,128)} %param.6) | copy-start | bytes 1572868
where the time goes:
time: 79.1 us; the launch traced here: 78.9 us
  Pallas kernels  73.4 us (93%)
  local copies, waits for them, and re-layouts  4.86 us (6%)
    pallas_call x1, Pallas kernels, fused(): pl.pallas_call(functools.partial(kernel, parts, samples, planes), out_sha...  73.4 us
    unnamed x13, local copies, waits for them, and re-layouts  4.86 us

commit v1 on v0

--- a/solution.py
+++ b/solution.py
@@ -193,8 +193,29 @@
     return lax.fori_loop(0, count // UNROLL, turn, carry)
 
 
-def rows_at(i, pieces, length):
-    return pl.ds(i, pieces, stride=length)
+def at_step(i):
+    return pl.ds(pl.multiple_of(i * SUBLANES, SUBLANES), SUBLANES)
+
+
+def gather_rows(ref, i, pieces, pitch):
+    tiles = [ref[j, pl.ds(i, pieces, stride=pitch), :] for j in range(ref.shape[0])]
+    groups = SUBLANES // pieces
+    count = len(tiles) // groups
+    tiles = [
+        tiles[j] if groups == 1
+        else jnp.concatenate([tiles[g * count + j] for g in range(groups)], axis=0)
+        for j in range(count)
+    ]
+    return jnp.concatenate(tiles, axis=1)
+
+
+def scatter_rows(ref, i, pieces, pitch, value):
+    groups = SUBLANES // pieces
+    count = ref.shape[0] // groups
+    for j in range(ref.shape[0]):
+        g, tile = j // count, j % count
+        ref[j, pl.ds(i, pieces, stride=pitch), :] = value[
+            g * pieces : (g + 1) * pieces, tile * LANES : (tile + 1) * LANES]
 
 
 def take(ref, at):
@@ -210,60 +231,55 @@
     return ref.shape[0] * LANES
 
 
-def factor_blocks(cond, factors, pieces, length, before, beyond, spread, drift):
+def factor_blocks(read, factors, length, before, beyond, spread, drift):
     low, up, inv, from_first, to_first = factors
-    shape = (pieces, width(cond))
-
-    def keep(i, d, ahead, state):
-        eta, eta_t, corner = state
-        r = 1.0 / d
+    shape = (SUBLANES, width(low))
+
+    def body(i, state):
+        here, behind, u, eta, eta_t, corner = state
+        after = read(jnp.minimum(i + 1, length - 1))
+        ahead = 2.0 * here * after / (here + after)
+        ahead = jnp.where(i == length - 1, last_face, ahead)
+        r = 1.0 / (1.0 + spread * (behind + ahead) + drift + (spread * behind + drift) * u)
         u = -spread * ahead * r
         lo = -(spread * ahead + drift) * r
-        at = rows_at(i, pieces, length)
+        first = eta * r
+        at = at_step(i)
         put(low, at, lo)
         put(up, at, u)
         put(inv, at, r)
-        first = eta * r
         put(from_first, at, first)
         put(to_first, at, eta_t * r)
-        return u, (-lo * eta, -u * eta_t, corner + first * eta_t)
-
-    def body(i, state):
-        here, behind, u, rest = state
-        after = take(cond, rows_at(jnp.minimum(i + 1, length - 1), pieces, length))
-        ahead = 2.0 * here * after / (here + after)
-        ahead = jnp.where(i == length - 1, last_face, ahead)
-        d = 1.0 + spread * (behind + ahead) + drift + (spread * behind + drift) * u
-        u, rest = keep(i, d, ahead, rest)
-        return after, ahead, u, rest
-
-    first_row = take(cond, rows_at(0, pieces, length))
-    last_face = beyond(first_row, take(cond, rows_at(length - 1, pieces, length)))
+        return after, ahead, u, -lo * eta, -u * eta_t, corner + first * eta_t
+
+    first_row = read(0)
+    last_face = beyond(first_row, read(length - 1))
     ones = jnp.ones(shape, jnp.float32)
     zeros = jnp.zeros(shape, jnp.float32)
-    state = steps(length, body, (first_row, before, zeros, (ones, ones, zeros)))
-    at = rows_at(length - 1, pieces, length)
-    return state[3][2], take(from_first, at), take(to_first, at), take(inv, at), last_face
-
-
-def sweep_down(values, out, low, inv, weights, pieces, length):
+    state = steps(length, body, (first_row, before, zeros, ones, ones, zeros))
+    at = at_step(length - 1)
+    return state[5], take(from_first, at), take(to_first, at), take(inv, at), last_face
+
+
+def sweep_down(read, out, low, inv, weights, length):
     def body(i, state):
         y, lo, total = state
-        at = rows_at(i, pieces, length)
-        y = take(values, at) - lo * y
+        at = at_step(i)
+        y = read(i) - lo * y
         put(out, at, y * take(inv, at))
         return y, take(low, at), total + take(weights, at) * y
 
-    zeros = jnp.zeros((pieces, width(values)), jnp.float32)
+    zeros = jnp.zeros((SUBLANES, width(low)), jnp.float32)
     _, _, total = steps(length, body, (zeros, zeros, zeros))
-    return total, take(out, rows_at(length - 1, pieces, length))
-
-
-def sweep_up(held, out, up, spike, incoming, following, pieces, length):
+    return total, take(out, at_step(length - 1))
+
+
+def sweep_up(held, write, up, spike, incoming, following, length):
     def body(k, x):
-        at = rows_at(length - 1 - k, pieces, length)
+        i = length - 1 - k
+        at = at_step(i)
         x = take(held, at) - take(spike, at) * incoming - take(up, at) * x
-        put(out, at, x)
+        write(i, x)
         return x
 
     steps(length, body, following)
@@ -275,19 +291,23 @@
     return s, vl + s * vf, r, r * vf, r * wf, wl + s * wf
 
 
-def tile_transpose(source, target):
+def tile_transpose(source, target, length, pitch, pitch_to):
     for i in range(target.shape[0]):
         for j in range(source.shape[0]):
-            target[i, j * LANES : (j + 1) * LANES, :] = source[j, i * LANES : (i + 1) * LANES, :].T
+            tile = jnp.concatenate(
+                [source[j, b * pitch : b * pitch + length, :] for b in (2 * i, 2 * i + 1)], axis=0).T
+            for half in range(2):
+                start = (2 * j + half) * pitch_to
+                target[i, start : start + length, :] = tile[half * length : (half + 1) * length, :]
 
 
 def kernel(
     parts, samples, planes,
-    conc, classes, conductivity, wells, control,
+    conc_in, classes_in, conductivity, wells, control,
     final_out, adjoint_out, gradient_out,
-    cond, cond_t, xl, xu, xi, xe, xf, yl, yu, yi, ye, yf, zu, zi,
-    field, held, field_t, held_t, later_t, source_t, final_t, adjoint_t,
-    hits_x, hits_y, halo_send, halo, corner, joint_x, joint_y, ends, ps, qs,
+    conc, classes, in_sem, cond, cond_t, xl, xu, xi, xe, xf, yl, yu, yi, ye, yf, zu, zi,
+    field, held, field_t, held_t, second_t, later_t, source_t, final_t, adjoint_t,
+    hits_x, hits_y, hits_step, halo_send, halo, corner, joint_x, joint_y, ends, ps, qs,
     landed, part_sum, sample_sum, term_sum, sample_term,
     send_sem, recv_sem, bulk_send, bulk_recv, sample_send, sample_recv, halo_ssem, halo_rsem,
 ):
@@ -297,6 +317,11 @@
     grid_cells = conc.shape[1]
     length_t = grid_cells // SUBLANES
     wide = conc.shape[0]
+    pitch, pitch_t = block + 1, length_t + 1
+    class_copy = pltpu.make_async_copy(classes_in, classes, in_sem.at[0])
+    class_copy.start()
+    conc_copy = pltpu.make_async_copy(conc_in, conc, in_sem.at[1])
+    conc_copy.start()
 
     barrier = pltpu.get_barrier_semaphore()
 
@@ -354,18 +379,33 @@
             copy.wait_recv()
         pending.extend(copies)
 
-    def fill(t, _):
-        at = pl.ds(pl.multiple_of(t * SUBLANES, SUBLANES), SUBLANES)
-        labels = classes[at, :]
-        values = jnp.full(labels.shape, conductivity[0], jnp.float32)
-        for label in range(1, conductivity.shape[0]):
-            values = jnp.where(labels == label, conductivity[label], values)
-        put(cond, at, values)
-        return 0
-
-    lax.fori_loop(0, wide // SUBLANES, fill, 0)
-    halo_send[0] = take(cond, rows_at(block - 1, planes, block))
-    halo_send[1] = take(cond, rows_at(0, planes, block))
+    class_copy.wait()
+
+    def x_rows(ref):
+        return lambda i: gather_rows(ref, i, planes, pitch)
+
+    def x_store(ref):
+        return lambda i, value: scatter_rows(ref, i, planes, pitch, value)
+
+    def y_rows(ref):
+        return lambda i: gather_rows(ref, i, SUBLANES, pitch_t)
+
+    def y_store(ref):
+        return lambda i, value: scatter_rows(ref, i, SUBLANES, pitch_t, value)
+
+    def in_order(ref):
+        return lambda i: take(ref, at_step(i))
+
+    for z in range(planes):
+        for t in range(0, block, SUBLANES):
+            labels = classes[z * block + t : z * block + t + SUBLANES, :]
+            values = jnp.full(labels.shape, conductivity[0], jnp.float32)
+            for label in range(1, conductivity.shape[0]):
+                values = jnp.where(labels == label, conductivity[label], values)
+            put(cond, slice(z * pitch + t, z * pitch + t + SUBLANES), values)
+    x_cond = x_rows(cond)
+    halo_send[0] = x_cond(block - 1)
+    halo_send[1] = x_cond(0)
     pl.semaphore_wait(barrier, parts - 1 + samples - 1)
     halo_copies = []
     for side, k in ((0, 1), (1, parts - 1)):
@@ -376,60 +416,60 @@
         copy.start()
         halo_copies.append(copy)
 
-    def factor_depth(t, _):
-        start = t * SUBLANES
-        here = take(cond, pl.ds(pl.multiple_of(start, SUBLANES), SUBLANES))
+    for t in range(0, block, SUBLANES):
+        here = take(cond, slice(t, t + SUBLANES))
         behind = jnp.zeros(here.shape, jnp.float32)
         u = behind
         for z in range(planes):
             if z < planes - 1:
-                after = take(cond, pl.ds(pl.multiple_of((z + 1) * block + start, SUBLANES), SUBLANES))
+                start = (z + 1) * pitch + t
+                after = take(cond, slice(start, start + SUBLANES))
                 ahead = 2.0 * here * after / (here + after)
             else:
                 after, ahead = here, jnp.zeros(here.shape, jnp.float32)
             r = 1.0 / (1.0 + spread_depth * (behind + ahead) + spread_depth * behind * u)
             u = -spread_depth * ahead * r
-            at = pl.ds(pl.multiple_of(z * block + start, SUBLANES), SUBLANES)
+            at = slice(z * block + t, z * block + t + SUBLANES)
             put(zi, at, r)
             put(zu, at, u)
             here, behind = after, ahead
-        return 0
-
-    lax.fori_loop(0, block // SUBLANES, factor_depth, 0)
-    tile_transpose(cond, cond_t)
+    tile_transpose(cond, cond_t, block, pitch, pitch_t)
 
     x_row = lax.broadcasted_iota(jnp.int32, hits_x.shape, 0) % block + me * block
     hits_x[...] = jnp.where(x_row == wells[0:1, :], 1.0, 0.0)
     y_row = lax.broadcasted_iota(jnp.int32, hits_y.shape, 0)
     hits_y[...] = jnp.where(y_row == wells[1:2, :], 1.0, 0.0)
+    y_row = y_row % SUBLANES * length_t + y_row // SUBLANES
+    hits_step[...] = jnp.where(y_row == wells[1:2, :], 1.0, 0.0)
     across_last = (((1,), (1,)), ((), ()))
     source = lax.dot_general(
         hits_x[0:block, :] * control[...], hits_y[...], across_last,
         precision=EXACT, preferred_element_type=jnp.float32)
+    conc_copy.wait()
     for z in range(planes):
         cut = slice(z * block, (z + 1) * block)
-        put(field, cut, conc[cut, :] + source)
+        put(field, slice(z * pitch, z * pitch + block), conc[cut, :] + source)
 
     arrive(halo_copies)
     x_factors = (xl, xu, xi, xe, xf)
     not_first = (me > 0).astype(jnp.float32)
     not_last = (me < parts - 1).astype(jnp.float32)
-    first_row = take(cond, rows_at(0, planes, block))
+    first_row = x_cond(0)
     face_before = not_first * 2.0 * halo[0] * first_row / (halo[0] + first_row)
 
     def beyond_x(first, last):
         return not_last * 2.0 * halo[1] * last / (halo[1] + last)
 
     corners = factor_blocks(
-        cond, x_factors, planes, block, face_before, beyond_x, spread_along, drift_along)
+        x_cond, x_factors, block, face_before, beyond_x, spread_along, drift_along)
     gff, glf, gfl, gll, face_ahead = corners
     for j, value in enumerate((gff, glf, gfl, gll, face_before, face_ahead)):
-        corner[me, j * planes : (j + 1) * planes, :] = value
+        corner[me, j * SUBLANES : (j + 1) * SUBLANES, :] = value
     corner_copies = spread_out(corner, 0)
 
     def ends_out(phase, first, last):
-        ends[phase, me, 0:planes, :] = first
-        ends[phase, me, planes : 2 * planes, :] = last
+        ends[phase, me, 0:SUBLANES, :] = first
+        ends[phase, me, SUBLANES : 2 * SUBLANES, :] = last
         copies = []
         for k in range(1, parts):
             copy = pltpu.make_async_remote_copy(
@@ -440,20 +480,20 @@
             copies.append(copy)
         return copies
 
-    def start_x(values, out, phase, flipped):
+    def start_x(read, out, phase, flipped):
         low, weights = (xu, xe) if flipped else (xl, xf)
-        first, last = sweep_down(values, out, low, xi, weights, planes, block)
+        first, last = sweep_down(read, out, low, xi, weights, block)
         return ends_out(phase, first, last)
 
-    def finish_x(copies, inner, out, phase, flipped):
+    def finish_x(copies, inner, write, phase, flipped):
         arrive(copies)
         way = 1 if flipped else 0
-        joint = lambda b, j: joint_x[way, b, j * planes : (j + 1) * planes, :]
-        firsts = [ends[phase, b, 0:planes, :] for b in range(parts)]
+        joint = lambda b, j: joint_x[way, b, j * SUBLANES : (j + 1) * SUBLANES, :]
+        firsts = [ends[phase, b, 0:SUBLANES, :] for b in range(parts)]
         alphas = []
         alpha = None
         for b in range(parts):
-            last = ends[phase, b, planes : 2 * planes, :]
+            last = ends[phase, b, SUBLANES : 2 * SUBLANES, :]
             alpha = last if b == 0 else last + joint(b, 0) * firsts[b] - joint(b, 1) * alpha
             alphas.append(alpha)
         zero = jnp.zeros_like(firsts[0])
@@ -471,14 +511,15 @@
         coupling = -spread_along * face_before if flipped else -(spread_along * face_before + drift_along)
         incoming = coupling * qs[me]
         up, spike = (xl, xf) if flipped else (xu, xe)
-        sweep_up(inner, out, up, spike, incoming, ps[me + 1], planes, block)
-
-    x1 = start_x(field, held, 0, False)
+        sweep_up(inner, write, up, spike, incoming, ps[me + 1], block)
+
+    x1 = start_x(x_rows(field), held, 0, False)
 
     row = lax.broadcasted_iota(jnp.int32, (SUBLANES, wide), 0)
     y_factors = (yl, yu, yi, ye, yf)
-    y_first = take(cond_t, rows_at(0, SUBLANES, length_t))
-    y_last = take(cond_t, rows_at(length_t - 1, SUBLANES, length_t))
+    y_cond = y_rows(cond_t)
+    y_first = y_cond(0)
+    y_last = y_cond(length_t - 1)
     last_before = pltpu.roll(y_last, 1, 0)
     y_before = jnp.where(row == 0, 0.0, 2.0 * last_before * y_first / (last_before + y_first))
 
@@ -487,7 +528,7 @@
         return jnp.where(row == SUBLANES - 1, 0.0, 2.0 * last * after / (last + after))
 
     gff, glf, gfl, gll, y_ahead = factor_blocks(
-        cond_t, y_factors, SUBLANES, length_t, y_before, beyond_y, spread_across, drift_across)
+        y_cond, y_factors, length_t, y_before, beyond_y, spread_across, drift_across)
     y_couplings = []
     for way in range(2):
         a = jnp.where(row == 0, 0.0, -(spread_across * y_before + drift_across))
@@ -518,11 +559,11 @@
                 row >= SUBLANES - 2 * distance, 0.0,
                 back * pltpu.roll(back, SUBLANES - distance, 0))
 
-    def solve_y(values, inner, out, flipped):
+    def solve_y(read, inner, write, flipped):
         way = 1 if flipped else 0
         low, weights = (yu, ye) if flipped else (yl, yf)
         up, spike = (yl, yf) if flipped else (yu, ye)
-        first, last = sweep_down(values, inner, low, yi, weights, SUBLANES, length_t)
+        first, last = sweep_down(read, inner, low, yi, weights, length_t)
         alpha = last + joint_y[way, 0] * first
         for level, distance in enumerate((1, 2, 4)):
             alpha = alpha + joint_y[way, 6 + level] * pltpu.roll(alpha, distance, 0)
@@ -534,33 +575,33 @@
         q = alpha - joint_y[way, 5] * p_next
         q_before = jnp.where(row == 0, 0.0, pltpu.roll(q, 1, 0))
         incoming = y_couplings[way] * q_before
-        sweep_up(inner, out, up, spike, incoming, p_next, SUBLANES, length_t)
+        sweep_up(inner, write, up, spike, incoming, p_next, length_t)
 
     def solve_z(values):
-        def body(t, _):
-            start = t * SUBLANES
-            ats = [pl.ds(pl.multiple_of(z * block + start, SUBLANES), SUBLANES) for z in range(planes)]
-            ys = [take(values, ats[0])]
+        for t in range(0, block, SUBLANES):
+            ats = [slice(z * block + t, z * block + t + SUBLANES) for z in range(planes)]
+            cells = [slice(z * pitch + t, z * pitch + t + SUBLANES) for z in range(planes)]
+            ys = [take(values, cells[0])]
             us = [take(zu, at) for at in ats]
             for z in range(1, planes):
-                ys.append(take(values, ats[z]) - us[z - 1] * ys[-1])
+                ys.append(take(values, cells[z]) - us[z - 1] * ys[-1])
             x = ys[-1] * take(zi, ats[-1])
-            put(values, ats[-1], x)
+            put(values, cells[-1], x)
             for z in range(planes - 2, -1, -1):
                 x = ys[z] * take(zi, ats[z]) - us[z] * x
-                put(values, ats[z], x)
-            return 0
-
-        lax.fori_loop(0, block // SUBLANES, body, 0)
-
-    put(source_t, slice(None), lax.dot_general(
+                put(values, cells[z], x)
+
+    source_turned = lax.dot_general(
         hits_y[...] * control[...], hits_x[...], across_last,
-        precision=EXACT, preferred_element_type=jnp.float32))
+        precision=EXACT, preferred_element_type=jnp.float32)
+    for b in range(SUBLANES):
+        put(source_t, slice(b * pitch_t, b * pitch_t + length_t),
+            source_turned[b * length_t : (b + 1) * length_t, :])
 
     arrive(corner_copies)
-    corner_of = lambda b, j: corner[b, j * planes : (j + 1) * planes, :]
+    corner_of = lambda b, j: corner[b, j * SUBLANES : (j + 1) * SUBLANES, :]
     for way in range(2):
-        beta = jnp.zeros((planes, grid_cells), jnp.float32)
+        beta = jnp.zeros((SUBLANES, corner.shape[2]), jnp.float32)
         for b in range(parts):
             gff, glf, gfl, gll, behind, ahead = [corner_of(b, j) for j in range(6)]
             a = -(spread_along * behind + drift_along) if b > 0 else jnp.zeros_like(behind)
@@ -572,46 +613,45 @@
                 terms = joint_terms(c * gff, c * gfl, a_next * glf, a_next * gll, beta)
             beta = terms[5]
             for j, value in enumerate(terms):
-                joint_x[way, b, j * planes : (j + 1) * planes, :] = value
-
-    finish_x(x1, held, field, 0, False)
+                joint_x[way, b, j * SUBLANES : (j + 1) * SUBLANES, :] = value
+
+    finish_x(x1, held, x_store(field), 0, False)
     solve_z(field)
-    tile_transpose(field, field_t)
-    solve_y(field_t, held_t, field_t, False)
-
-    field_t[...] = field_t[...] + source_t[...]
-    solve_y(field_t, held_t, field_t, False)
-    tile_transpose(field_t, field)
+    tile_transpose(field, field_t, block, pitch, pitch_t)
+    with_source = lambda i, value: put(second_t, at_step(i), value + y_rows(source_t)(i))
+    solve_y(y_rows(field_t), held_t, with_source, False)
+
+    solve_y(in_order(second_t), held_t, y_store(field_t), False)
+    tile_transpose(field_t, field, length_t, pitch_t, pitch)
     solve_z(field)
-    x2 = start_x(field, held, 1, False)
-    finish_x(x2, held, field, 1, False)
-
-    x3 = start_x(field, held, 2, True)
-    tile_transpose(field, final_t)
+    x2 = start_x(x_rows(field), held, 1, False)
+    finish_x(x2, held, x_store(field), 1, False)
+
+    x3 = start_x(x_rows(field), held, 2, True)
+    tile_transpose(field, final_t, block, pitch, length_t)
     final_copies = send_blocks(final_t, 0)
 
-    def squares(t, total):
-        value = take(field, pl.ds(pl.multiple_of(t * SUBLANES, SUBLANES), SUBLANES))
-        return total + value * value
-
-    total = lax.fori_loop(
-        0, wide // SUBLANES, squares, jnp.zeros((SUBLANES, grid_cells), jnp.float32))
+    total = jnp.zeros((SUBLANES, grid_cells), jnp.float32)
+    for z in range(planes):
+        for t in range(0, block, SUBLANES):
+            value = take(field, slice(z * pitch + t, z * pitch + t + SUBLANES))
+            total = total + value * value
     part_sum[me] = 0.5 * sum(
         total[:, j : j + LANES] for j in range(0, grid_cells, LANES))
     misfit_copies = spread_out(part_sum, 5)
 
-    finish_x(x3, held, field, 2, True)
+    finish_x(x3, held, x_store(field), 2, True)
     solve_z(field)
-    tile_transpose(field, field_t)
-    solve_y(field_t, held_t, later_t, True)
+    tile_transpose(field, field_t, block, pitch, pitch_t)
+    solve_y(y_rows(field_t), held_t, lambda i, value: put(later_t, at_step(i), value), True)
     arrive(misfit_copies)
     sample_sum[own] = sum(part_sum[b] for b in range(parts))
     sample_copies = spread_samples(sample_sum, 0)
 
-    solve_y(later_t, held_t, field_t, True)
-    tile_transpose(field_t, field)
+    solve_y(in_order(later_t), held_t, y_store(field_t), True)
+    tile_transpose(field_t, field, length_t, pitch_t, pitch)
     solve_z(field)
-    x4 = start_x(field, held, 3, True)
+    x4 = start_x(x_rows(field), held, 3, True)
     half = lax.broadcasted_iota(jnp.int32, (block, LANES), 1) < block
 
     def assemble(phase, out):
@@ -625,8 +665,8 @@
 
     arrive(final_copies)
     assemble(0, final_out)
-    finish_x(x4, held, field, 3, True)
-    tile_transpose(field, adjoint_t)
+    finish_x(x4, held, x_store(field), 3, True)
+    tile_transpose(field, adjoint_t, block, pitch, length_t)
     adjoint_copies = send_blocks(adjoint_t, 1)
 
     arrive(sample_copies)
@@ -635,8 +675,11 @@
     own_misfit = jnp.sum(sample_sum[own], keepdims=True)
     weight = (1.0 + aversion * (own_misfit - average) / (average + epsilon)) / samples
     picked = jnp.dot(
-        take(later_t, slice(None)) + take(adjoint_t, slice(None)), hits_x[...],
+        take(adjoint_t, slice(None)), hits_x[...],
         precision=EXACT, preferred_element_type=jnp.float32) * hits_y[...]
+    picked = picked + jnp.dot(
+        take(later_t, slice(None)), hits_x[...],
+        precision=EXACT, preferred_element_type=jnp.float32) * hits_step[...]
     picked = picked.reshape(grid_cells // SUBLANES, SUBLANES, picked.shape[1])
     term_sum[me] = weight * jnp.sum(picked, axis=0)
     term_copies = spread_out(term_sum, 6)
@@ -658,19 +701,27 @@
     count = wells.shape[1]
     f32 = jnp.float32
     vmem = lambda *shape: pltpu.VMEM(shape, f32)
-    flat, turned = (grid_cells // LANES, wide, LANES), (wide // LANES, grid_cells, LANES)
+    length_t = grid_cells // SUBLANES
+    step = wide * grid_cells // block // SUBLANES
+    flat = (grid_cells // LANES, planes * (block + 1), LANES)
+    flat_even = (grid_cells // LANES, wide, LANES)
+    turned = (wide // LANES, SUBLANES * (length_t + 1), LANES)
+    turned_even = (wide // LANES, grid_cells, LANES)
+    ordered = (step // LANES, block * SUBLANES, LANES)
     dma = pltpu.SemaphoreType.DMA
-    scratch = [vmem(*flat), vmem(*turned)]
-    scratch += [vmem(*flat)] * 5 + [vmem(*turned)] * 5 + [vmem(*flat)] * 2
-    scratch += [vmem(*flat)] * 2 + [vmem(*turned)] * 6
+    scratch = [vmem(wide, grid_cells), pltpu.VMEM((wide, grid_cells), jnp.int32), dma((2,))]
+    scratch += [vmem(*flat), vmem(*turned)]
+    scratch += [vmem(*ordered)] * 5 + [vmem(*turned_even)] * 5 + [vmem(*flat_even)] * 2
+    scratch += [vmem(*flat), vmem(*ordered), vmem(*turned), vmem(*turned_even)]
+    scratch += [vmem(*turned_even)] * 2 + [vmem(*turned)] + [vmem(*turned_even)] * 2
     scratch += [
-        vmem(wide, count), vmem(grid_cells, count),
-        vmem(2, planes, grid_cells), vmem(2, planes, grid_cells),
-        vmem(parts, 6 * planes, grid_cells),
-        vmem(2, parts, 6 * planes, grid_cells),
+        vmem(wide, count), vmem(grid_cells, count), vmem(grid_cells, count),
+        vmem(2, SUBLANES, step), vmem(2, SUBLANES, step),
+        vmem(parts, 6 * SUBLANES, step),
+        vmem(2, parts, 6 * SUBLANES, step),
         vmem(2, 12, SUBLANES, wide),
-        vmem(4, parts, 2 * planes, grid_cells),
-        vmem(parts + 1, planes, grid_cells), vmem(parts + 1, planes, grid_cells),
+        vmem(4, parts, 2 * SUBLANES, step),
+        vmem(parts + 1, SUBLANES, step), vmem(parts + 1, SUBLANES, step),
         vmem(2, parts, wide // LANES, block, LANES),
         vmem(parts, SUBLANES, LANES), vmem(samples, SUBLANES, LANES),
         vmem(parts, SUBLANES, count), vmem(samples, SUBLANES, count),
@@ -678,12 +729,13 @@
         dma((2, samples)), dma((2, samples)), dma((2,)), dma((2,)),
     ]
     on_vmem = pl.BlockSpec(memory_space=pltpu.VMEM)
+    anywhere = pl.BlockSpec(memory_space=pl.ANY)
     on_smem = pl.BlockSpec(memory_space=pltpu.SMEM)
     out = jax.ShapeDtypeStruct((planes, block, grid_cells), f32)
     final, adjoint, gradient = pl.pallas_call(
         functools.partial(kernel, parts, samples, planes),
         out_shape=(out, out, jax.ShapeDtypeStruct((1, count), f32)),
-        in_specs=[on_vmem, on_vmem, on_smem, on_vmem, on_vmem],
+        in_specs=[anywhere, anywhere, on_smem, on_vmem, on_vmem],
         out_specs=(on_vmem, on_vmem, on_vmem),
         scratch_shapes=scratch,
         compiler_params=pltpu.CompilerParams(
@@ -700,7 +752,8 @@
     fits = (
         2 * block == LANES and planes % 2 == 0 and parts % 2 == 0 and parts > 1
         and parts * block == grid_cells and grid_cells % LANES == 0
-        and (planes * block) % LANES == 0
+        and (planes * block) % LANES == 0 and SUBLANES % planes == 0
+        and (planes * grid_cells) % (SUBLANES * LANES) == 0 and grid_cells // SUBLANES == block
     )
     if fits:
         return fused(parts, samples, concentration, classes, conductivity, wells, control)

time: 79.1 us -> 57.2 us (0.72)
  Pallas kernels: 73.4 us -> 51.4 us
    pallas_call x1, Pallas kernels: 73.4 us -> 51.4 us  [fused(): pl.pallas_call(functools.partial(kernel, parts, samples, planes), out_sha...]
where the time goes in v1:
time: 57.2 us; the launch traced here: 56.9 us
  Pallas kernels  51.4 us (90%)
  local copies, waits for them, and re-layouts  4.86 us (8%)
  between operations  0.67 us (1%)
    pallas_call x1, Pallas kernels, fused(): pl.pallas_call(functools.partial(kernel, parts, samples, planes), out_sha...  51.4 us
    unnamed x13, local copies, waits for them, and re-layouts  4.86 us

profile of v1, /device:TPU:0, one launch (start us, length us, event | category | flops | bytes accessed | tf_op | source)
XLA Modules:
  0.0 56.9 jit_solution(11521230142475976704)
XLA Ops:
  0.6 0.0 copy-start.4
  0.6 0.0 copy-start.2
  0.7 0.0 copy-start.3
  0.7 0.6 %copy-done.4 = f32[64]{0:T(128)S(1)} copy-done((f32[64]{0:T(128)S(1)}, f32[64]{0:T(128)}, u32[]{:S(2)}) %copy-start.4) | copy-done | bytes 280
  1.3 0.0 copy-done.2
  1.3 0.0 copy-done.3
  1.3 0.0 copy-start
  1.3 1.0 %copy-done = f32[1,4,64,512]{3,2,1,0:T(8,128)S(1)} copy-done((f32[1,4,64,512]{3,2,1,0:T(8,128)S(1)}, f32[1,4,64,512]{3,2,1,0:T(8,128)}, u32[]{:S(2)}) %copy-start) | copy-done | bytes 524312
  2.4 0.0 copy-start.1
  2.4 1.0 %copy-done.1 = s32[1,4,64,512]{3,2,1,0:T(8,128)S(1)} copy-done((s32[1,4,64,512]{3,2,1,0:T(8,128)S(1)}, s32[1,4,64,512]{3,2,1,0:T(8,128)}, u32[]{:S(2)}) %copy-start.1) | copy-done | bytes 524312
  3.4 51.4 %shard_map.76 = (f32[4,64,512]{2,1,0:T(8,128)S(1)}, f32[4,64,512]{2,1,0:T(8,128)S(1)}, f32[1,64]{1,0:T(1,128)S(1)}) custom-call(f32[256,512]{1,0:T(8,128)S(1)} %bitcast.6, s32[256,512]{1,0:T(8,128)S(1)} %bitcast.7, f32[16]{0:T(128)S(1)} %copy-done.3, s32[2,64]{1,0:T(2,128)S(1)} %copy-done.2, f32[1,64]{1,0:T(1,128)S(1)} %bitcast.10), custom_call_target="tpu_custom_call" | custom-call | tf_op jit(solution)/shard_map/pallas_call | solution.py:735
  54.8 0.8 %copy.11 = f32[1,4,64,512]{3,2,1,0:T(8,128)} copy(f32[1,4,64,512]{3,2,1,0:T(8,128)S(1)} %bitcast.9) | data formatting | bytes 1048576
  55.6 0.8 %copy.12 = f32[1,4,64,512]{3,2,1,0:T(8,128)} copy(f32[1,4,64,512]{3,2,1,0:T(8,128)S(1)} %bitcast.8) | data formatting | bytes 1048576
  56.4 0.5 copy.13
Async XLA Ops:
  0.6 0.7 %copy-start.4 = (f32[64]{0:T(128)S(1)}, f32[64]{0:T(128)}, u32[]{:S(2)}) copy-start(f32[64]{0:T(128)} %param.9) | copy-start | bytes 772
  0.6 0.7 %copy-start.2 = (s32[2,64]{1,0:T(2,128)S(1)}, s32[2,64]{1,0:T(2,128)}, u32[]{:S(2)}) copy-start(s32[2,64]{1,0:T(2,128)} %wells.1) | copy-start | bytes 1540
  0.7 0.7 %copy-start.3 = (f32[16]{0:T(128)S(1)}, f32[16]{0:T(128)}, u32[]{:S(2)}) copy-start(f32[16]{0:T(128)} %conductivity.1) | copy-start | bytes 196
  1.3 1.0 %copy-start = (f32[1,4,64,512]{3,2,1,0:T(8,128)S(1)}, f32[1,4,64,512]{3,2,1,0:T(8,128)}, u32[]{:S(2)}) copy-start(f32[1,4,64,512]{3,2,1,0:T(8,128)} %param.5) | copy-start | bytes 1572868
  2.4 1.0 %copy-start.1 = (s32[1,4,64,512]{3,2,1,0:T(8,128)S(1)}, s32[1,4,64,512]{3,2,1,0:T(8,128)}, u32[]{:S(2)}) copy-start(s32[1,4,64,512]{3,2,1,0:T(8,128)} %param.6) | copy-start | bytes 1572868

commit v2 on v1

--- a/solution.py
+++ b/solution.py
@@ -184,10 +184,16 @@
 EXACT = lax.Precision.HIGHEST
 
 
-def steps(count, body, carry):
+def steps(count, load, work, store, carry):
     def turn(t, state):
-        for k in range(UNROLL):
-            state = body(t * UNROLL + k, state)
+        group = [t * UNROLL + k for k in range(UNROLL)]
+        loaded = [load(i) for i in group]
+        results = []
+        for i, values in zip(group, loaded):
+            state, result = work(i, state, values)
+            results.append(result)
+        for i, result in zip(group, results):
+            store(i, result)
         return state
 
     return lax.fori_loop(0, count // UNROLL, turn, carry)
@@ -197,25 +203,12 @@
     return pl.ds(pl.multiple_of(i * SUBLANES, SUBLANES), SUBLANES)
 
 
-def gather_rows(ref, i, pieces, pitch):
-    tiles = [ref[j, pl.ds(i, pieces, stride=pitch), :] for j in range(ref.shape[0])]
-    groups = SUBLANES // pieces
-    count = len(tiles) // groups
-    tiles = [
-        tiles[j] if groups == 1
-        else jnp.concatenate([tiles[g * count + j] for g in range(groups)], axis=0)
-        for j in range(count)
-    ]
-    return jnp.concatenate(tiles, axis=1)
-
-
-def scatter_rows(ref, i, pieces, pitch, value):
-    groups = SUBLANES // pieces
-    count = ref.shape[0] // groups
-    for j in range(ref.shape[0]):
-        g, tile = j // count, j % count
-        ref[j, pl.ds(i, pieces, stride=pitch), :] = value[
-            g * pieces : (g + 1) * pieces, tile * LANES : (tile + 1) * LANES]
+def gather_rows(ref, i, pitch):
+    return take(ref, pl.ds(i, SUBLANES, stride=pitch))
+
+
+def scatter_rows(ref, i, pitch, value):
+    put(ref, pl.ds(i, SUBLANES, stride=pitch), value)
 
 
 def take(ref, at):
@@ -231,58 +224,76 @@
     return ref.shape[0] * LANES
 
 
-def factor_blocks(read, factors, length, before, beyond, spread, drift):
-    low, up, inv, from_first, to_first = factors
-    shape = (SUBLANES, width(low))
-
-    def body(i, state):
-        here, behind, u, eta, eta_t, corner = state
-        after = read(jnp.minimum(i + 1, length - 1))
-        ahead = 2.0 * here * after / (here + after)
-        ahead = jnp.where(i == length - 1, last_face, ahead)
-        r = 1.0 / (1.0 + spread * (behind + ahead) + drift + (spread * behind + drift) * u)
-        u = -spread * ahead * r
-        lo = -(spread * ahead + drift) * r
-        first = eta * r
+def factor_blocks(lines, length):
+    def load(i):
+        return [line[0](jnp.minimum(i + 1, length - 1)) for line in lines]
+
+    def work(i, states, loaded):
+        new_states, results = [], []
+        for (_, _, _, last_face, spread, drift), state, after in zip(lines, states, loaded):
+            here, behind, u, eta, eta_t, corner = state
+            ahead = 2.0 * here * after / (here + after)
+            ahead = jnp.where(i == length - 1, last_face, ahead)
+            r = 1.0 / (1.0 + spread * (behind + ahead) + drift + (spread * behind + drift) * u)
+            u = -spread * ahead * r
+            lo = -(spread * ahead + drift) * r
+            first = eta * r
+            new_states.append((after, ahead, u, -lo * eta, -u * eta_t, corner + first * eta_t))
+            results.append((lo, u, r, first, eta_t * r))
+        return new_states, results
+
+    def store(i, results):
+        for line, result in zip(lines, results):
+            for ref, value in zip(line[1], result):
+                put(ref, at_step(i), value)
+
+    start = []
+    for read, factors, before, _, _, _ in lines:
+        ones = jnp.ones((SUBLANES, width(factors[0])), jnp.float32)
+        zeros = jnp.zeros_like(ones)
+        start.append((read(0), before, zeros, ones, ones, zeros))
+    states = steps(length, load, work, store, start)
+    at = at_step(length - 1)
+    corners = []
+    for line, state in zip(lines, states):
+        _, _, inv, from_first, to_first = line[1]
+        corners.append((state[5], take(from_first, at), take(to_first, at), take(inv, at)))
+    return corners
+
+
+def sweep_down(read, out, low, inv, weights, length):
+    def load(i):
         at = at_step(i)
-        put(low, at, lo)
-        put(up, at, u)
-        put(inv, at, r)
-        put(from_first, at, first)
-        put(to_first, at, eta_t * r)
-        return after, ahead, u, -lo * eta, -u * eta_t, corner + first * eta_t
-
-    first_row = read(0)
-    last_face = beyond(first_row, read(length - 1))
-    ones = jnp.ones(shape, jnp.float32)
-    zeros = jnp.zeros(shape, jnp.float32)
-    state = steps(length, body, (first_row, before, zeros, ones, ones, zeros))
-    at = at_step(length - 1)
-    return state[5], take(from_first, at), take(to_first, at), take(inv, at), last_face
-
-
-def sweep_down(read, out, low, inv, weights, length):
-    def body(i, state):
+        return read(i), take(inv, at), take(low, at), take(weights, at)
+
+    def work(i, state, values):
         y, lo, total = state
-        at = at_step(i)
-        y = read(i) - lo * y
-        put(out, at, y * take(inv, at))
-        return y, take(low, at), total + take(weights, at) * y
+        here, r, lo_next, share = values
+        y = here - lo * y
+        return (y, lo_next, total + share * y), y * r
+
+    def store(i, z):
+        put(out, at_step(i), z)
 
     zeros = jnp.zeros((SUBLANES, width(low)), jnp.float32)
-    _, _, total = steps(length, body, (zeros, zeros, zeros))
+    _, _, total = steps(length, load, work, store, (zeros, zeros, zeros))
     return total, take(out, at_step(length - 1))
 
 
 def sweep_up(held, write, up, spike, incoming, following, length):
-    def body(k, x):
-        i = length - 1 - k
-        at = at_step(i)
-        x = take(held, at) - take(spike, at) * incoming - take(up, at) * x
-        write(i, x)
-        return x
-
-    steps(length, body, following)
+    def load(k):
+        at = at_step(length - 1 - k)
+        return take(held, at), take(spike, at), take(up, at)
+
+    def work(k, x, values):
+        here, share, factor = values
+        x = here - share * incoming - factor * x
+        return x, x
+
+    def store(k, x):
+        write(length - 1 - k, x)
+
+    steps(length, load, work, store, following)
 
 
 def joint_terms(vf, vl, wf, wl, beta):
@@ -291,14 +302,29 @@
     return s, vl + s * vf, r, r * vf, r * wf, wl + s * wf
 
 
-def tile_transpose(source, target, length, pitch, pitch_to):
+def turn_over(source, target, planes, length, pitch, pitch_to):
+    tiles = source.shape[0]
     for i in range(target.shape[0]):
-        for j in range(source.shape[0]):
+        for j in range(target.shape[1] // pitch_to // 2):
+            first = j // tiles * planes + 2 * i
             tile = jnp.concatenate(
-                [source[j, b * pitch : b * pitch + length, :] for b in (2 * i, 2 * i + 1)], axis=0).T
+                [source[j % tiles, b * pitch : b * pitch + length, :] for b in (first, first + 1)],
+                axis=0).T
             for half in range(2):
                 start = (2 * j + half) * pitch_to
                 target[i, start : start + length, :] = tile[half * length : (half + 1) * length, :]
+
+
+def turn_back(source, target, planes, length, pitch, pitch_to):
+    tiles = target.shape[0]
+    for i in range(source.shape[0]):
+        for j in range(source.shape[1] // pitch // 2):
+            tile = jnp.concatenate(
+                [source[i, b * pitch : b * pitch + length, :] for b in (2 * j, 2 * j + 1)], axis=0).T
+            for half in range(2):
+                start = (j // tiles * planes + 2 * i + half) * pitch_to
+                target[j % tiles, start : start + length, :] = tile[
+                    half * length : (half + 1) * length, :]
 
 
 def kernel(
@@ -382,27 +408,32 @@
     class_copy.wait()
 
     def x_rows(ref):
-        return lambda i: gather_rows(ref, i, planes, pitch)
+        return lambda i: gather_rows(ref, i, pitch)
 
     def x_store(ref):
-        return lambda i, value: scatter_rows(ref, i, planes, pitch, value)
+        return lambda i, value: scatter_rows(ref, i, pitch, value)
 
     def y_rows(ref):
-        return lambda i: gather_rows(ref, i, SUBLANES, pitch_t)
+        return lambda i: gather_rows(ref, i, pitch_t)
 
     def y_store(ref):
-        return lambda i, value: scatter_rows(ref, i, SUBLANES, pitch_t, value)
+        return lambda i, value: scatter_rows(ref, i, pitch_t, value)
 
     def in_order(ref):
         return lambda i: take(ref, at_step(i))
 
-    for z in range(planes):
-        for t in range(0, block, SUBLANES):
-            labels = classes[z * block + t : z * block + t + SUBLANES, :]
-            values = jnp.full(labels.shape, conductivity[0], jnp.float32)
-            for label in range(1, conductivity.shape[0]):
-                values = jnp.where(labels == label, conductivity[label], values)
-            put(cond, slice(z * pitch + t, z * pitch + t + SUBLANES), values)
+    groups = SUBLANES // planes
+    columns = grid_cells // groups
+    for g in range(groups):
+        for z in range(planes):
+            for t in range(0, block, SUBLANES):
+                start = z * block + t
+                labels = classes[start : start + SUBLANES, g * columns : (g + 1) * columns]
+                values = jnp.full(labels.shape, conductivity[0], jnp.float32)
+                for label in range(1, conductivity.shape[0]):
+                    values = jnp.where(labels == label, conductivity[label], values)
+                start = (g * planes + z) * pitch + t
+                put(cond, slice(start, start + SUBLANES), values)
     x_cond = x_rows(cond)
     halo_send[0] = x_cond(block - 1)
     halo_send[1] = x_cond(0)
@@ -416,24 +447,25 @@
         copy.start()
         halo_copies.append(copy)
 
-    for t in range(0, block, SUBLANES):
-        here = take(cond, slice(t, t + SUBLANES))
+    for g, t in [(g, t) for g in range(groups) for t in range(0, block, SUBLANES)]:
+        start = g * planes * pitch + t
+        here = take(cond, slice(start, start + SUBLANES))
         behind = jnp.zeros(here.shape, jnp.float32)
         u = behind
         for z in range(planes):
             if z < planes - 1:
-                start = (z + 1) * pitch + t
+                start = (g * planes + z + 1) * pitch + t
                 after = take(cond, slice(start, start + SUBLANES))
                 ahead = 2.0 * here * after / (here + after)
             else:
                 after, ahead = here, jnp.zeros(here.shape, jnp.float32)
             r = 1.0 / (1.0 + spread_depth * (behind + ahead) + spread_depth * behind * u)
             u = -spread_depth * ahead * r
-            at = slice(z * block + t, z * block + t + SUBLANES)
-            put(zi, at, r)
-            put(zu, at, u)
+            start = (g * planes + z) * block + t
+            put(zi, slice(start, start + SUBLANES), r)
+            put(zu, slice(start, start + SUBLANES), u)
             here, behind = after, ahead
-    tile_transpose(cond, cond_t, block, pitch, pitch_t)
+    turn_over(cond, cond_t, planes, block, pitch, pitch_t)
 
     x_row = lax.broadcasted_iota(jnp.int32, hits_x.shape, 0) % block + me * block
     hits_x[...] = jnp.where(x_row == wells[0:1, :], 1.0, 0.0)
@@ -446,9 +478,23 @@
         hits_x[0:block, :] * control[...], hits_y[...], across_last,
         precision=EXACT, preferred_element_type=jnp.float32)
     conc_copy.wait()
-    for z in range(planes):
-        cut = slice(z * block, (z + 1) * block)
-        put(field, slice(z * pitch, z * pitch + block), conc[cut, :] + source)
+    for g in range(groups):
+        cut = slice(g * columns, (g + 1) * columns)
+        for z in range(planes):
+            start = (g * planes + z) * pitch
+            put(field, slice(start, start + block),
+                conc[z * block : (z + 1) * block, cut] + source[:, cut])
+
+    row = lax.broadcasted_iota(jnp.int32, (SUBLANES, wide), 0)
+    y_factors = (yl, yu, yi, ye, yf)
+    y_cond = y_rows(cond_t)
+    y_first = y_cond(0)
+    y_last = y_cond(length_t - 1)
+    last_before = pltpu.roll(y_last, 1, 0)
+    y_before = jnp.where(row == 0, 0.0, 2.0 * last_before * y_first / (last_before + y_first))
+
+    first_after = pltpu.roll(y_first, SUBLANES - 1, 0)
+    y_ahead = jnp.where(row == SUBLANES - 1, 0.0, 2.0 * y_last * first_after / (y_last + first_after))
 
     arrive(halo_copies)
     x_factors = (xl, xu, xi, xe, xf)
@@ -457,12 +503,13 @@
     first_row = x_cond(0)
     face_before = not_first * 2.0 * halo[0] * first_row / (halo[0] + first_row)
 
-    def beyond_x(first, last):
-        return not_last * 2.0 * halo[1] * last / (halo[1] + last)
-
-    corners = factor_blocks(
-        x_cond, x_factors, block, face_before, beyond_x, spread_along, drift_along)
-    gff, glf, gfl, gll, face_ahead = corners
+    last_row = x_cond(block - 1)
+    face_ahead = not_last * 2.0 * halo[1] * last_row / (halo[1] + last_row)
+    (gff, glf, gfl, gll), y_corners = factor_blocks(
+        (
+            (x_cond, x_factors, face_before, face_ahead, spread_along, drift_along),
+            (y_cond, y_factors, y_before, y_ahead, spread_across, drift_across),
+        ), block)
     for j, value in enumerate((gff, glf, gfl, gll, face_before, face_ahead)):
         corner[me, j * SUBLANES : (j + 1) * SUBLANES, :] = value
     corner_copies = spread_out(corner, 0)
@@ -515,20 +562,7 @@
 
     x1 = start_x(x_rows(field), held, 0, False)
 
-    row = lax.broadcasted_iota(jnp.int32, (SUBLANES, wide), 0)
-    y_factors = (yl, yu, yi, ye, yf)
-    y_cond = y_rows(cond_t)
-    y_first = y_cond(0)
-    y_last = y_cond(length_t - 1)
-    last_before = pltpu.roll(y_last, 1, 0)
-    y_before = jnp.where(row == 0, 0.0, 2.0 * last_before * y_first / (last_before + y_first))
-
-    def beyond_y(first, last):
-        after = pltpu.roll(first, SUBLANES - 1, 0)
-        return jnp.where(row == SUBLANES - 1, 0.0, 2.0 * last * after / (last + after))
-
-    gff, glf, gfl, gll, y_ahead = factor_blocks(
-        y_cond, y_factors, length_t, y_before, beyond_y, spread_across, drift_across)
+    gff, glf, gfl, gll = y_corners
     y_couplings = []
     for way in range(2):
         a = jnp.where(row == 0, 0.0, -(spread_across * y_before + drift_across))
@@ -578,9 +612,11 @@
         sweep_up(inner, write, up, spike, incoming, p_next, length_t)
 
     def solve_z(values):
-        for t in range(0, block, SUBLANES):
-            ats = [slice(z * block + t, z * block + t + SUBLANES) for z in range(planes)]
-            cells = [slice(z * pitch + t, z * pitch + t + SUBLANES) for z in range(planes)]
+        for g, t in [(g, t) for g in range(groups) for t in range(0, block, SUBLANES)]:
+            ats = [(g * planes + z) * block + t for z in range(planes)]
+            cells = [(g * planes + z) * pitch + t for z in range(planes)]
+            ats = [slice(start, start + SUBLANES) for start in ats]
+            cells = [slice(start, start + SUBLANES) for start in cells]
             ys = [take(values, cells[0])]
             us = [take(zu, at) for at in ats]
             for z in range(1, planes):
@@ -617,39 +653,38 @@
 
     finish_x(x1, held, x_store(field), 0, False)
     solve_z(field)
-    tile_transpose(field, field_t, block, pitch, pitch_t)
+    turn_over(field, field_t, planes, block, pitch, pitch_t)
     with_source = lambda i, value: put(second_t, at_step(i), value + y_rows(source_t)(i))
     solve_y(y_rows(field_t), held_t, with_source, False)
 
     solve_y(in_order(second_t), held_t, y_store(field_t), False)
-    tile_transpose(field_t, field, length_t, pitch_t, pitch)
+    turn_back(field_t, field, planes, length_t, pitch_t, pitch)
     solve_z(field)
     x2 = start_x(x_rows(field), held, 1, False)
     finish_x(x2, held, x_store(field), 1, False)
 
     x3 = start_x(x_rows(field), held, 2, True)
-    tile_transpose(field, final_t, block, pitch, length_t)
+    turn_over(field, final_t, planes, block, pitch, length_t)
     final_copies = send_blocks(final_t, 0)
 
-    total = jnp.zeros((SUBLANES, grid_cells), jnp.float32)
-    for z in range(planes):
+    total = jnp.zeros((SUBLANES, columns), jnp.float32)
+    for b in range(SUBLANES):
         for t in range(0, block, SUBLANES):
-            value = take(field, slice(z * pitch + t, z * pitch + t + SUBLANES))
+            value = take(field, slice(b * pitch + t, b * pitch + t + SUBLANES))
             total = total + value * value
-    part_sum[me] = 0.5 * sum(
-        total[:, j : j + LANES] for j in range(0, grid_cells, LANES))
+    part_sum[me] = 0.5 * sum(total[:, j : j + LANES] for j in range(0, columns, LANES))
     misfit_copies = spread_out(part_sum, 5)
 
     finish_x(x3, held, x_store(field), 2, True)
     solve_z(field)
-    tile_transpose(field, field_t, block, pitch, pitch_t)
+    turn_over(field, field_t, planes, block, pitch, pitch_t)
     solve_y(y_rows(field_t), held_t, lambda i, value: put(later_t, at_step(i), value), True)
     arrive(misfit_copies)
     sample_sum[own] = sum(part_sum[b] for b in range(parts))
     sample_copies = spread_samples(sample_sum, 0)
 
     solve_y(in_order(later_t), held_t, y_store(field_t), True)
-    tile_transpose(field_t, field, length_t, pitch_t, pitch)
+    turn_back(field_t, field, planes, length_t, pitch_t, pitch)
     solve_z(field)
     x4 = start_x(x_rows(field), held, 3, True)
     half = lax.broadcasted_iota(jnp.int32, (block, LANES), 1) < block
@@ -666,7 +701,7 @@
     arrive(final_copies)
     assemble(0, final_out)
     finish_x(x4, held, x_store(field), 3, True)
-    tile_transpose(field, adjoint_t, block, pitch, length_t)
+    turn_over(field, adjoint_t, planes, block, pitch, length_t)
     adjoint_copies = send_blocks(adjoint_t, 1)
 
     arrive(sample_copies)
@@ -703,8 +738,8 @@
     vmem = lambda *shape: pltpu.VMEM(shape, f32)
     length_t = grid_cells // SUBLANES
     step = wide * grid_cells // block // SUBLANES
-    flat = (grid_cells // LANES, planes * (block + 1), LANES)
-    flat_even = (grid_cells // LANES, wide, LANES)
+    flat = (step // LANES, SUBLANES * (block + 1), LANES)
+    flat_even = (step // LANES, SUBLANES * block, LANES)
     turned = (wide // LANES, SUBLANES * (length_t + 1), LANES)
     turned_even = (wide // LANES, grid_cells, LANES)
     ordered = (step // LANES, block * SUBLANES, LANES)
@@ -729,7 +764,7 @@
         dma((2, samples)), dma((2, samples)), dma((2,)), dma((2,)),
     ]
     on_vmem = pl.BlockSpec(memory_space=pltpu.VMEM)
-    anywhere = pl.BlockSpec(memory_space=pl.ANY)
+    anywhere = pl.BlockSpec(memory_space=pltpu.HBM)
     on_smem = pl.BlockSpec(memory_space=pltpu.SMEM)
     out = jax.ShapeDtypeStruct((planes, block, grid_cells), f32)
     final, adjoint, gradient = pl.pallas_call(

time: 57.2 us -> 57.4 us (level)
  no operation moved by 1% of the time
where the time goes in v2:
time: 57.4 us; the launch traced here: 57.1 us
  Pallas kernels  51.6 us (90%)
  local copies, waits for them, and re-layouts  4.86 us (8%)
  between operations  0.67 us (1%)
    pallas_call x1, Pallas kernels, fused(): pl.pallas_call(functools.partial(kernel, parts, samples, planes), out_sha...  51.6 us
    unnamed x13, local copies, waits for them, and re-layouts  4.86 us

profile of v2, /device:TPU:0, one launch (start us, length us, event | category | flops | bytes accessed | tf_op | source)
XLA Modules:
  0.0 57.1 jit_solution(13553536727730327866)
XLA Ops:
  0.6 0.0 copy-start.4
  0.6 0.0 copy-start.2
  0.7 0.0 copy-start.3
  0.7 0.6 %copy-done.4 = f32[64]{0:T(128)S(1)} copy-done((f32[64]{0:T(128)S(1)}, f32[64]{0:T(128)}, u32[]{:S(2)}) %copy-start.4) | copy-done | bytes 280
  1.3 0.0 copy-done.2
  1.3 0.0 copy-done.3
  1.3 0.0 copy-start
  1.3 1.0 %copy-done = f32[1,4,64,512]{3,2,1,0:T(8,128)S(1)} copy-done((f32[1,4,64,512]{3,2,1,0:T(8,128)S(1)}, f32[1,4,64,512]{3,2,1,0:T(8,128)}, u32[]{:S(2)}) %copy-start) | copy-done | bytes 524312
  2.4 0.0 copy-start.1
  2.4 1.0 %copy-done.1 = s32[1,4,64,512]{3,2,1,0:T(8,128)S(1)} copy-done((s32[1,4,64,512]{3,2,1,0:T(8,128)S(1)}, s32[1,4,64,512]{3,2,1,0:T(8,128)}, u32[]{:S(2)}) %copy-start.1) | copy-done | bytes 524312
  3.4 51.6 %shard_map.76 = (f32[4,64,512]{2,1,0:T(8,128)S(1)}, f32[4,64,512]{2,1,0:T(8,128)S(1)}, f32[1,64]{1,0:T(1,128)S(1)}) custom-call(f32[256,512]{1,0:T(8,128)S(1)} %bitcast.6, s32[256,512]{1,0:T(8,128)S(1)} %bitcast.7, f32[16]{0:T(128)S(1)} %copy-done.3, s32[2,64]{1,0:T(2,128)S(1)} %copy-done.2, f32[1,64]{1,0:T(1,128)S(1)} %bitcast.10), custom_call_target="tpu_custom_call" | custom-call | tf_op jit(solution)/shard_map/pallas_call | solution.py:770
  55.0 0.8 %copy.11 = f32[1,4,64,512]{3,2,1,0:T(8,128)} copy(f32[1,4,64,512]{3,2,1,0:T(8,128)S(1)} %bitcast.9) | data formatting | bytes 1048576
  55.8 0.8 %copy.12 = f32[1,4,64,512]{3,2,1,0:T(8,128)} copy(f32[1,4,64,512]{3,2,1,0:T(8,128)S(1)} %bitcast.8) | data formatting | bytes 1048576
  56.6 0.5 copy.13
Async XLA Ops:
  0.6 0.7 %copy-start.4 = (f32[64]{0:T(128)S(1)}, f32[64]{0:T(128)}, u32[]{:S(2)}) copy-start(f32[64]{0:T(128)} %param.9) | copy-start | bytes 772
  0.6 0.7 %copy-start.2 = (s32[2,64]{1,0:T(2,128)S(1)}, s32[2,64]{1,0:T(2,128)}, u32[]{:S(2)}) copy-start(s32[2,64]{1,0:T(2,128)} %wells.1) | copy-start | bytes 1540
  0.7 0.7 %copy-start.3 = (f32[16]{0:T(128)S(1)}, f32[16]{0:T(128)}, u32[]{:S(2)}) copy-start(f32[16]{0:T(128)} %conductivity.1) | copy-start | bytes 196
  1.3 1.0 %copy-start = (f32[1,4,64,512]{3,2,1,0:T(8,128)S(1)}, f32[1,4,64,512]{3,2,1,0:T(8,128)}, u32[]{:S(2)}) copy-start(f32[1,4,64,512]{3,2,1,0:T(8,128)} %param.5) | copy-start | bytes 1572868
  2.4 1.0 %copy-start.1 = (s32[1,4,64,512]{3,2,1,0:T(8,128)S(1)}, s32[1,4,64,512]{3,2,1,0:T(8,128)}, u32[]{:S(2)}) copy-start(s32[1,4,64,512]{3,2,1,0:T(8,128)} %param.6) | copy-start | bytes 1572868

commit v3 on v2

--- a/solution.py
+++ b/solution.py
@@ -180,23 +180,34 @@
 LANES = 128
 SUBLANES = 8
 UNROLL = 8
+TURN = 16
 MESH = pl.DeviceIdType.MESH
 EXACT = lax.Precision.HIGHEST
 
 
+def inverse(x):
+    r = pl.reciprocal(x, approx=True)
+    r = r * (2.0 - x * r)
+    return r * (2.0 - x * r)
+
+
 def steps(count, load, work, store, carry):
     def turn(t, state):
-        group = [t * UNROLL + k for k in range(UNROLL)]
-        loaded = [load(i) for i in group]
-        results = []
-        for i, values in zip(group, loaded):
-            state, result = work(i, state, values)
-            results.append(result)
-        for i, result in zip(group, results):
+        waiting = []
+        for first in range(0, TURN, UNROLL):
+            group = [t * TURN + first + k for k in range(UNROLL)]
+            loaded = [load(i) for i in group]
+            for i, result in waiting:
+                store(i, result)
+            waiting = []
+            for i, values in zip(group, loaded):
+                state, result = work(i, state, values)
+                waiting.append((i, result))
+        for i, result in waiting:
             store(i, result)
         return state
 
-    return lax.fori_loop(0, count // UNROLL, turn, carry)
+    return lax.fori_loop(0, count // TURN, turn, carry)
 
 
 def at_step(i):
@@ -232,9 +243,9 @@
         new_states, results = [], []
         for (_, _, _, last_face, spread, drift), state, after in zip(lines, states, loaded):
             here, behind, u, eta, eta_t, corner = state
-            ahead = 2.0 * here * after / (here + after)
+            ahead = 2.0 * here * after * inverse(here + after)
             ahead = jnp.where(i == length - 1, last_face, ahead)
-            r = 1.0 / (1.0 + spread * (behind + ahead) + drift + (spread * behind + drift) * u)
+            r = inverse(1.0 + spread * (behind + ahead) + drift + (spread * behind + drift) * u)
             u = -spread * ahead * r
             lo = -(spread * ahead + drift) * r
             first = eta * r
@@ -297,7 +308,7 @@
 
 
 def joint_terms(vf, vl, wf, wl, beta):
-    r = 1.0 / (1.0 - vf * beta)
+    r = inverse(1.0 - vf * beta)
     s = vl * beta * r
     return s, vl + s * vf, r, r * vf, r * wf, wl + s * wf
 
@@ -447,24 +458,6 @@
         copy.start()
         halo_copies.append(copy)
 
-    for g, t in [(g, t) for g in range(groups) for t in range(0, block, SUBLANES)]:
-        start = g * planes * pitch + t
-        here = take(cond, slice(start, start + SUBLANES))
-        behind = jnp.zeros(here.shape, jnp.float32)
-        u = behind
-        for z in range(planes):
-            if z < planes - 1:
-                start = (g * planes + z + 1) * pitch + t
-                after = take(cond, slice(start, start + SUBLANES))
-                ahead = 2.0 * here * after / (here + after)
-            else:
-                after, ahead = here, jnp.zeros(here.shape, jnp.float32)
-            r = 1.0 / (1.0 + spread_depth * (behind + ahead) + spread_depth * behind * u)
-            u = -spread_depth * ahead * r
-            start = (g * planes + z) * block + t
-            put(zi, slice(start, start + SUBLANES), r)
-            put(zu, slice(start, start + SUBLANES), u)
-            here, behind = after, ahead
     turn_over(cond, cond_t, planes, block, pitch, pitch_t)
 
     x_row = lax.broadcasted_iota(jnp.int32, hits_x.shape, 0) % block + me * block
@@ -561,6 +554,25 @@
         sweep_up(inner, write, up, spike, incoming, ps[me + 1], block)
 
     x1 = start_x(x_rows(field), held, 0, False)
+
+    for g, t in [(g, t) for g in range(groups) for t in range(0, block, SUBLANES)]:
+        start = g * planes * pitch + t
+        here = take(cond, slice(start, start + SUBLANES))
+        behind = jnp.zeros(here.shape, jnp.float32)
+        u = behind
+        for z in range(planes):
+            if z < planes - 1:
+                start = (g * planes + z + 1) * pitch + t
+                after = take(cond, slice(start, start + SUBLANES))
+                ahead = 2.0 * here * after * inverse(here + after)
+            else:
+                after, ahead = here, jnp.zeros(here.shape, jnp.float32)
+            r = inverse(1.0 + spread_depth * (behind + ahead) + spread_depth * behind * u)
+            u = -spread_depth * ahead * r
+            start = (g * planes + z) * block + t
+            put(zi, slice(start, start + SUBLANES), r)
+            put(zu, slice(start, start + SUBLANES), u)
+            here, behind = after, ahead
 
     gff, glf, gfl, gll = y_corners
     y_couplings = []
@@ -774,7 +786,7 @@
         out_specs=(on_vmem, on_vmem, on_vmem),
         scratch_shapes=scratch,
         compiler_params=pltpu.CompilerParams(
-            collective_id=0, has_side_effects=True, vmem_limit_bytes=48 * 1024 * 1024),
+            collective_id=0, has_side_effects=True, vmem_limit_bytes=63 * 1024 * 1024),
     )(
         concentration.reshape(wide, grid_cells), classes.reshape(wide, grid_cells), conductivity, wells,
         control.reshape(1, count))

time: 57.4 us -> 56.9 us (level)
  local copies, waits for them, and re-layouts: 4.86 us -> 3.24 us
  Pallas kernels: 51.6 us -> 52.8 us
    unnamed x13 -> x7, local copies, waits for them, and re-layouts: 4.86 us -> 3.24 us
    pallas_call x1, Pallas kernels: 51.6 us -> 52.8 us  [fused(): pl.pallas_call(functools.partial(kernel, parts, samples, planes), out_sha...]
where the time goes in v3:
time: 56.9 us; the launch traced here: 56.7 us
  Pallas kernels  52.8 us (93%)
  local copies, waits for them, and re-layouts  3.24 us (6%)
  between operations  0.65 us (1%)
    pallas_call x1, Pallas kernels, fused(): pl.pallas_call(functools.partial(kernel, parts, samples, planes), out_sha...  52.8 us
    unnamed x7, local copies, waits for them, and re-layouts  3.24 us

profile of v3, /device:TPU:0, one launch (start us, length us, event | category | flops | bytes accessed | tf_op | source)
XLA Modules:
  0.0 56.7 jit_solution(5707712485708226047)
XLA Ops:
  0.6 52.8 %shard_map.76 = (f32[4,64,512]{2,1,0:T(8,128)}, f32[4,64,512]{2,1,0:T(8,128)}, f32[1,64]{1,0:T(1,128)}) custom-call(f32[256,512]{1,0:T(8,128)} %bitcast.6, s32[256,512]{1,0:T(8,128)} %bitcast.7, f32[16]{0:T(128)} %conductivity.1, s32[2,64]{1,0:T(2,128)} %wells.1, f32[1,64]{1,0:T(1,128)} %bitcast.10), custom_call_target="tpu_custom_call" | custom-call | tf_op jit(solution)/shard_map/pallas_call | solution.py:782
  53.4 0.0 copy-start
  53.5 1.9 %copy.11 = f32[1,4,64,512]{3,2,1,0:T(8,128)} copy(f32[1,4,64,512]{3,2,1,0:T(8,128)} %bitcast.9) | data formatting | bytes 1048576
  55.4 0.0 copy-done
  55.4 0.0 copy-start.1
  55.4 0.8 %copy.12 = f32[1,4,64,512]{3,2,1,0:T(8,128)} copy(f32[1,4,64,512]{3,2,1,0:T(8,128)S(1)} %bitcast.8) | data formatting | bytes 1048576
  56.2 0.0 copy-done.1
  56.2 0.5 copy.13
Async XLA Ops:
  53.4 1.9 %copy-start = (f32[4,64,512]{2,1,0:T(8,128)S(1)}, f32[4,64,512]{2,1,0:T(8,128)}, u32[]{:S(2)}) copy-start(f32[4,64,512]{2,1,0:T(8,128)} %get-tuple-element.7) | copy-start | bytes 1572868
  55.4 0.8 %copy-start.1 = (f32[1,64]{1,0:T(1,128)S(1)}, f32[1,64]{1,0:T(1,128)}, u32[]{:S(2)}) copy-start(f32[1,64]{1,0:T(1,128)} %get-tuple-element.8) | copy-start | bytes 772
